TPU v7x, 32 devices: a whole 2x2x4 slice. The times are simulated.
32 devices in a mesh: shard: 4 (over z), head: 4 (over x, core), tensor: 2 (over y).
Axes of the slice: x: 2, y: 2, z: 4, core: 2. Of those that a mesh axis runs over, the one named last changes fastest.
Arguments:
- block_input: bfloat16 [192, 197, 512], P(('shard', 'head', 'tensor')), may hold values from -6 to 6
- cotangent: bfloat16 [192, 197, 512], P(('shard', 'head', 'tensor')), may hold values from -6 to 6
- routes: int32 [192, 197, 2], P(('shard', 'head', 'tensor')), may hold values from 0 to 3, all different within a row; in each aligned block of 1182 rows (0 to 1181, 1182 to 2363, ..., all dimensions but the last counted through in order) at most 738 rows name the same one
- priority: int32 [32, 2364], P(('shard', 'head', 'tensor')), may hold values from 0 to 2363, each once within a row
- norm_params: float32 [4, 512], replicated, may hold values from -0.4 to 1.3, as said below
- norm_moment: float32 [4, 512], replicated, may hold values from -112 to 112
- norm_square: float32 [4, 512], replicated, may hold values from 12.10368 to 192.9024
- qkv_weight: float32 [512, 3, 512], P(('shard', 'tensor'), None, 'head'), may hold values from -0.3125 to 0.3125
- qkv_moment: float32 [512, 3, 512], P(('shard', 'tensor'), None, 'head'), may hold values from -128 to 128
- qkv_square: float32 [512, 3, 512], P(('shard', 'tensor'), None, 'head'), may hold values from 18.912 to 302.592
- attn_weight: float32 [512, 512], P('head', ('shard', 'tensor')), may hold values from -0.75 to 0.75
- attn_moment: float32 [512, 512], P('head', ('shard', 'tensor')), may hold values from -48 to 48
- attn_square: float32 [512, 512], P('head', ('shard', 'tensor')), may hold values from 3.02592 to 49.1712
- router_weight: float32 [512, 4], replicated, may hold values from -0.1875 to 0.1875
- router_moment: float32 [512, 4], replicated, may hold values from -1024 to 1024
- router_square: float32 [512, 4], replicated, may hold values from 1210.368 to 19365.889
- expert_in: float32 [4, 512, 2048], P('shard', 'head', 'tensor'), may hold values from -0.25 to 0.25
- in_moment: float32 [4, 512, 2048], P('shard', 'head', 'tensor'), may hold values from -16 to 16
- in_square: float32 [4, 512, 2048], P('shard', 'head', 'tensor'), may hold values from 0.37824 to 6.05184
- expert_out: float32 [4, 2048, 512], P('shard', 'tensor', 'head'), may hold values from -0.4375 to 0.4375
- out_moment: float32 [4, 2048, 512], P('shard', 'tensor', 'head'), may hold values from -14 to 14
- out_square: float32 [4, 2048, 512], P('shard', 'tensor', 'head'), may hold values from 0.21276 to 3.4278
Outputs:
- block_output: bfloat16 [192, 197, 512], P(('shard', 'head', 'tensor'))
- input_grad: float32 [192, 197, 512], P(('shard', 'head', 'tensor'))
- new_norm: float32 [4, 512], replicated
- new_norm_moment: float32 [4, 512], replicated
- new_norm_square: float32 [4, 512], replicated
- new_qkv: float32 [512, 3, 512], P(('shard', 'tensor'), None, 'head')
- new_qkv_moment: float32 [512, 3, 512], P(('shard', 'tensor'), None, 'head')
- new_qkv_square: float32 [512, 3, 512], P(('shard', 'tensor'), None, 'head')
- new_attn: float32 [512, 512], P('head', ('shard', 'tensor'))
- new_attn_moment: float32 [512, 512], P('head', ('shard', 'tensor'))
- new_attn_square: float32 [512, 512], P('head', ('shard', 'tensor'))
- new_router: float32 [512, 4], replicated
- new_router_moment: float32 [512, 4], replicated
- new_router_square: float32 [512, 4], replicated
- new_in: float32 [4, 512, 2048], P('shard', 'head', 'tensor')
- new_in_moment: float32 [4, 512, 2048], P('shard', 'head', 'tensor')
- new_in_square: float32 [4, 512, 2048], P('shard', 'head', 'tensor')
- new_out: float32 [4, 2048, 512], P('shard', 'tensor', 'head')
- new_out_moment: float32 [4, 2048, 512], P('shard', 'tensor', 'head')
- new_out_square: float32 [4, 2048, 512], P('shard', 'tensor', 'head')
Inputs may be any that keep to these rules, and one draw needn't show every extreme that they name: `routes`: A token's two experts differ; among the tokens of one routing group no expert is named more than 738 times. `priority`: row g ranks the pairs of routing group g (the tokens of images g * 6 to g * 6 + 5); pair 2 t + k is route k of the group's t-th token; each rank appears once. `norm_params`: rows 0 and 2 are the two norms' gains, rows 1 and 3 their biases.
All inputs are finite; a program needn't handle non-finite values.
Results may differ from a plain program's by a relative error of at most 0.025.
Values may be sent and summed in bfloat16 or wider, within the bound.
No kernel may reach another device: no remote copies, remote signals or barrier semaphores. Data moves between devices by JAX's collectives and lax.ppermute only.
A program may use at most 192 MiB of HBM per device.

v0:
```python
from functools import partial

import jax
import jax.numpy as jnp
from jax import lax
from jax.sharding import PartitionSpec as P

HEAD_DIM = 64
FF = 2048
STEP = 10


EPS_NORM = 1e-06
BETA_ONE = 0.9
BETA_TWO = 0.999
ADAM_EPS = 1e-08
DECAY_RATE = 0.1


def norm_forward(values, gain_row, bias_row):
    center = jnp.mean(values, axis=-1, keepdims=True)
    shifted = values - center
    inverse = lax.rsqrt(jnp.mean(shifted * shifted, axis=-1, keepdims=True) + EPS_NORM)
    unit_rows = shifted * inverse
    return (unit_rows * gain_row + bias_row, unit_rows, inverse)


def norm_backward(grad_rows, unit_rows, inverse, gain_row):
    scaled = grad_rows * gain_row
    inner_grad = (
        scaled
        - jnp.mean(scaled, axis=-1, keepdims=True)
        - unit_rows * jnp.mean(scaled * unit_rows, axis=-1, keepdims=True)
    )
    return (
        inner_grad * inverse,
        jnp.sum(grad_rows * unit_rows, axis=0),
        jnp.sum(grad_rows, axis=0),
    )


def gelu_grad(pre_act, upstream):
    result, pullback = jax.vjp(partial(jax.nn.gelu, approximate=True), pre_act)
    return pullback(upstream)[0]


def adam_update(weight, gradient, moment, square, step_rate, decay_rate):
    moment_new = BETA_ONE * moment + (1.0 - BETA_ONE) * gradient
    square_new = BETA_TWO * square + (1.0 - BETA_TWO) * gradient * gradient
    first_hat = moment_new / (1.0 - BETA_ONE**STEP)
    second_hat = square_new / (1.0 - BETA_TWO**STEP)
    weight_new = weight - step_rate * (
        first_hat / (jnp.sqrt(second_hat) + ADAM_EPS) + decay_rate * weight
    )
    return (weight_new, moment_new, square_new)


def send_rows(parcel):
    copies = jnp.broadcast_to(
        parcel[:, None], (parcel.shape[0], lax.axis_size("tensor")) + parcel.shape[1:]
    )
    flat_copies = copies.reshape((-1,) + parcel.shape[1:])
    arrived = lax.all_to_all(
        flat_copies, ("shard", "tensor"), split_axis=0, concat_axis=0, tiled=True
    )
    return arrived.reshape(copies.shape)


def return_rows(partial_rows):
    flat_rows = partial_rows.reshape((-1,) + partial_rows.shape[2:])
    arrived = lax.all_to_all(
        flat_rows.astype(jnp.bfloat16), ("shard", "tensor"), split_axis=0, concat_axis=0, tiled=True
    ).astype(flat_rows.dtype)
    return jnp.sum(arrived.reshape(partial_rows.shape), axis=1)


def on_device(
    block_input,
    cotangent,
    routes,
    priority,
    norm_params,
    norm_moment,
    norm_square,
    qkv_weight,
    qkv_moment,
    qkv_square,
    attn_weight,
    attn_moment,
    attn_square,
    router_weight,
    router_moment,
    router_square,
    expert_in,
    in_moment,
    in_square,
    expert_out,
    out_moment,
    out_square,
):
    images, length, model_width = block_input.shape
    row_count = images * length
    local_experts = expert_in.shape[0]
    shards = lax.axis_size("shard")
    experts = local_experts * shards
    capacity = 9 * row_count // (4 * experts)
    score_scale = HEAD_DIM ** (-0.5)
    full_qkv, full_attn = (
        lax.all_gather(qkv_weight.astype(jnp.bfloat16), ("shard", "tensor"), axis=0, tiled=True),
        lax.all_gather(attn_weight.astype(jnp.bfloat16), ("shard", "tensor"), axis=1, tiled=True),
    )
    inputs = block_input.astype(jnp.float32).reshape(row_count, model_width)
    normed, unit_one, inverse_one = norm_forward(inputs, norm_params[0], norm_params[1])
    normed_low = normed.astype(jnp.bfloat16).reshape(images, length, model_width)
    gathered, hidden_in, hidden_out = (
        lax.all_gather(normed_low, "head", axis=0, tiled=True),
        lax.all_gather(expert_in.astype(jnp.bfloat16), "head", axis=1, tiled=True),
        lax.all_gather(expert_out.astype(jnp.bfloat16), "head", axis=2, tiled=True),
    )
    local_heads = full_qkv.shape[2] // HEAD_DIM
    all_images = gathered.shape[0]
    head_shape = (all_images, length, local_heads, HEAD_DIM)
    projected = jnp.einsum(
        "isd,dcn->iscn", gathered, full_qkv, preferred_element_type=jnp.float32
    ).astype(jnp.bfloat16)
    queries = projected[:, :, 0].reshape(head_shape)
    key_rows = projected[:, :, 1].reshape(head_shape)
    value_rows = projected[:, :, 2].reshape(head_shape)
    scores = (
        jnp.einsum("iqhe,ikhe->ihqk", queries, key_rows, preferred_element_type=jnp.float32)
        * score_scale
    )
    score_top = jnp.max(scores, axis=-1, keepdims=True)
    log_total = score_top + jnp.log(jnp.sum(jnp.exp(scores - score_top), axis=-1, keepdims=True))
    probs_low = jnp.exp(scores - log_total).astype(jnp.bfloat16)
    context = jnp.einsum(
        "ihqk,ikhe->iqhe", probs_low, value_rows, preferred_element_type=jnp.float32
    ).astype(jnp.bfloat16)
    context = context.reshape(all_images * length, local_heads * HEAD_DIM)
    attended = lax.psum_scatter(
        jnp.dot(context, full_attn, preferred_element_type=jnp.float32).astype(jnp.bfloat16),
        "head",
        scatter_dimension=0,
        tiled=True,
    ).astype(jnp.float32)
    hidden = inputs + attended
    normed_two, unit_two, inverse_two = norm_forward(hidden, norm_params[2], norm_params[3])
    second_low = normed_two.astype(jnp.bfloat16)
    router_low = router_weight.astype(jnp.bfloat16)
    logits = jnp.dot(second_low, router_low, preferred_element_type=jnp.float32)
    route_probs = jax.nn.softmax(logits, axis=-1)
    route_hot = (
        routes.reshape(row_count, 2)[:, :, None]
        == jnp.arange(experts, dtype=jnp.int32)[None, None, :]
    ).astype(jnp.float32)
    gate_values = jnp.sum(route_probs[:, None, :] * route_hot, axis=-1)
    expert_ids = routes.reshape(2 * row_count)
    rank_values = priority[0]
    pair_hot = route_hot.reshape(2 * row_count, experts)
    earlier = (rank_values[None, :] < rank_values[:, None]).astype(jnp.bfloat16)
    counts = jnp.dot(earlier, pair_hot.astype(jnp.bfloat16), preferred_element_type=jnp.float32)
    slot_index = jnp.sum(counts * pair_hot, axis=1).astype(jnp.int32)
    target = jnp.where(
        slot_index < capacity, expert_ids * capacity + slot_index, experts * capacity
    )
    filler = jnp.full((experts * capacity,), 2 * row_count, jnp.int32)
    owner_pair = filler.at[target].set(jnp.arange(2 * row_count, dtype=jnp.int32), mode="drop")
    padded = jnp.concatenate([second_low, jnp.zeros((1, model_width), jnp.bfloat16)], axis=0)
    parcel = padded[owner_pair // 2].reshape(shards, local_experts, capacity, model_width)
    arrived = send_rows(parcel)
    pre_act = jnp.einsum("stecd,edf->stecf", arrived, hidden_in, preferred_element_type=jnp.float32)
    active = jax.nn.gelu(pre_act, approximate=True).astype(jnp.bfloat16)
    part_rows = jnp.einsum(
        "stecf,efd->stecd", active, hidden_out, preferred_element_type=jnp.float32
    )
    expert_rows = return_rows(part_rows).reshape(experts * capacity, model_width)
    padded_out = jnp.concatenate([expert_rows, jnp.zeros((1, model_width), jnp.float32)], axis=0)
    per_pair = padded_out[target].reshape(row_count, 2, model_width)
    block_sum = hidden + jnp.sum(gate_values[:, :, None] * per_pair, axis=1)
    block_output = block_sum.astype(jnp.bfloat16).reshape(images, length, model_width)
    upstream = cotangent.astype(jnp.float32).reshape(row_count, model_width)
    pair_grad = (
        (gate_values[:, :, None] * upstream[:, None, :])
        .astype(jnp.bfloat16)
        .reshape(2 * row_count, model_width)
    )
    gate_grad = jnp.sum(upstream[:, None, :] * per_pair, axis=-1)
    padded_grad = jnp.concatenate([pair_grad, jnp.zeros((1, model_width), jnp.bfloat16)], axis=0)
    grad_parcel = padded_grad[owner_pair].reshape(shards, local_experts, capacity, model_width)
    grad_arrived = send_rows(grad_parcel)
    grad_out_part = jnp.einsum(
        "stecf,stecd->efd", active, grad_arrived, preferred_element_type=jnp.float32
    )
    active_grad = jnp.einsum(
        "stecd,efd->stecf", grad_arrived, hidden_out, preferred_element_type=jnp.float32
    )
    pre_grad = gelu_grad(pre_act, active_grad).astype(jnp.bfloat16)
    grad_in_part = jnp.einsum(
        "stecd,stecf->edf", arrived, pre_grad, preferred_element_type=jnp.float32
    )
    row_grad = jnp.einsum(
        "stecf,edf->stecd", pre_grad, hidden_in, preferred_element_type=jnp.float32
    )
    slot_grad = return_rows(row_grad).reshape(experts * capacity, model_width)
    padded_slot = jnp.concatenate([slot_grad, jnp.zeros((1, model_width), jnp.float32)], axis=0)
    second_grad = jnp.sum(padded_slot[target].reshape(row_count, 2, model_width), axis=1)
    prob_sum = jnp.sum(gate_grad[:, :, None] * route_hot, axis=1)
    logit_grad = (
        route_probs * (prob_sum - jnp.sum(route_probs * prob_sum, axis=-1, keepdims=True))
    ).astype(jnp.bfloat16)
    router_grad = jnp.einsum(
        "rd,re->de", second_low, logit_grad, preferred_element_type=jnp.float32
    )
    second_grad = second_grad + jnp.einsum(
        "re,de->rd", logit_grad, router_low, preferred_element_type=jnp.float32
    )
    hidden_part, gain_two, bias_two = norm_backward(
        second_grad, unit_two, inverse_two, norm_params[2]
    )
    hidden_grad = upstream + hidden_part
    attended_grad = lax.all_gather(hidden_grad.astype(jnp.bfloat16), "head", axis=0, tiled=True)
    attn_grad = jnp.einsum("rn,rd->nd", context, attended_grad, preferred_element_type=jnp.float32)
    context_grad = jnp.einsum(
        "rd,nd->rn", attended_grad, full_attn, preferred_element_type=jnp.float32
    ).astype(jnp.bfloat16)
    context_grad = context_grad.reshape(head_shape)
    scores_again = (
        jnp.einsum("iqhe,ikhe->ihqk", queries, key_rows, preferred_element_type=jnp.float32)
        * score_scale
    )
    probs_full = jnp.exp(scores_again - log_total)
    prob_grad = jnp.einsum(
        "iqhe,ikhe->ihqk", context_grad, value_rows, preferred_element_type=jnp.float32
    )
    score_grad = (
        probs_full * (prob_grad - jnp.sum(probs_full * prob_grad, axis=-1, keepdims=True))
    ).astype(jnp.bfloat16)
    query_grad = (
        jnp.einsum("ihqk,ikhe->iqhe", score_grad, key_rows, preferred_element_type=jnp.float32)
        * score_scale
    )
    key_grad = (
        jnp.einsum("ihqk,iqhe->ikhe", score_grad, queries, preferred_element_type=jnp.float32)
        * score_scale
    )
    value_grad = jnp.einsum(
        "ihqk,iqhe->ikhe", probs_low, context_grad, preferred_element_type=jnp.float32
    )
    projected_grad = (
        jnp.stack([query_grad, key_grad, value_grad], axis=2)
        .reshape(all_images, length, 3, local_heads * HEAD_DIM)
        .astype(jnp.bfloat16)
    )
    qkv_grad = jnp.einsum(
        "isd,iscn->dcn", gathered, projected_grad, preferred_element_type=jnp.float32
    )
    normed_part = jnp.einsum(
        "iscn,dcn->isd", projected_grad, full_qkv, preferred_element_type=jnp.float32
    )
    normed_grad, in_grad, out_grad = (
        lax.psum_scatter(
            normed_part.astype(jnp.bfloat16), "head", scatter_dimension=0, tiled=True
        ).astype(jnp.float32),
        lax.psum_scatter(
            grad_in_part.astype(jnp.bfloat16), "head", scatter_dimension=1, tiled=True
        ).astype(jnp.float32),
        lax.psum_scatter(
            grad_out_part.astype(jnp.bfloat16), "head", scatter_dimension=2, tiled=True
        ).astype(jnp.float32),
    )
    input_part, gain_one, bias_one = norm_backward(
        normed_grad.reshape(row_count, model_width), unit_one, inverse_one, norm_params[0]
    )
    input_grad = (hidden_grad + input_part).reshape(images, length, model_width)
    norm_grad = jnp.stack([gain_one, bias_one, gain_two, bias_two])
    norm_grad, router_grad = lax.psum((norm_grad, router_grad), ("shard", "head", "tensor"))
    qkv_grad, attn_grad = (
        lax.psum_scatter(qkv_grad, ("shard", "tensor"), scatter_dimension=0, tiled=True),
        lax.psum_scatter(attn_grad, ("shard", "tensor"), scatter_dimension=1, tiled=True),
    )
    norm_new = adam_update(norm_params, norm_grad, norm_moment, norm_square, 0.25, 0.0)
    qkv_new = adam_update(
        qkv_weight, qkv_grad, qkv_moment, qkv_square, 1.3 * model_width ** (-0.5), DECAY_RATE
    )
    attn_new = adam_update(
        attn_weight, attn_grad, attn_moment, attn_square, 3.0 * model_width ** (-0.5), DECAY_RATE
    )
    router_new = adam_update(
        router_weight,
        router_grad,
        router_moment,
        router_square,
        0.75 * model_width ** (-0.5),
        DECAY_RATE,
    )
    in_new = adam_update(
        expert_in, in_grad, in_moment, in_square, 1.0 * model_width ** (-0.5), DECAY_RATE
    )
    out_new = adam_update(
        expert_out, out_grad, out_moment, out_square, 0.8 * experts * FF ** (-0.5), DECAY_RATE
    )
    return (
        block_output,
        input_grad,
        norm_new[0],
        norm_new[1],
        norm_new[2],
        qkv_new[0],
        qkv_new[1],
        qkv_new[2],
        attn_new[0],
        attn_new[1],
        attn_new[2],
        router_new[0],
        router_new[1],
        router_new[2],
        in_new[0],
        in_new[1],
        in_new[2],
        out_new[0],
        out_new[1],
        out_new[2],
    )


def solution(mesh):
    return jax.shard_map(
        on_device,
        mesh=mesh,
        in_specs=(
            P(("shard", "head", "tensor"), None, None),
            P(("shard", "head", "tensor"), None, None),
            P(("shard", "head", "tensor"), None, None),
            P(("shard", "head", "tensor"), None),
            P(),
            P(),
            P(),
            P(("shard", "tensor"), None, "head"),
            P(("shard", "tensor"), None, "head"),
            P(("shard", "tensor"), None, "head"),
            P("head", ("shard", "tensor")),
            P("head", ("shard", "tensor")),
            P("head", ("shard", "tensor")),
            P(),
            P(),
            P(),
            P("shard", "head", "tensor"),
            P("shard", "head", "tensor"),
            P("shard", "head", "tensor"),
            P("shard", "tensor", "head"),
            P("shard", "tensor", "head"),
            P("shard", "tensor", "head"),
        ),
        out_specs=(
            P(("shard", "head", "tensor"), None, None),
            P(("shard", "head", "tensor"), None, None),
            P(),
            P(),
            P(),
            P(("shard", "tensor"), None, "head"),
            P(("shard", "tensor"), None, "head"),
            P(("shard", "tensor"), None, "head"),
            P("head", ("shard", "tensor")),
            P("head", ("shard", "tensor")),
            P("head", ("shard", "tensor")),
            P(),
            P(),
            P(),
            P("shard", "head", "tensor"),
            P("shard", "head", "tensor"),
            P("shard", "head", "tensor"),
            P("shard", "tensor", "head"),
            P("shard", "tensor", "head"),
            P("shard", "tensor", "head"),
        ),
        check_vma=False,
    )
```

profile of v0, /device:TPU:0, one launch (start us, length us, event | category | flops | bytes accessed | tf_op | source)
XLA Modules:
  0.0 1206.1 jit_solution(14683179083162993930)
XLA Ops:
  15.8 3.6 fusion.73
  20.1 12.3 %scatter_custom_fusion = s32[2656]{0:T(1024)S(1)} fusion(s32[2364]{0:T(1024)S(1)} %get-tuple-element.31, s32[2364]{0:T(1024)S(1)} %iota.8, s32[]{:T(128)} %constant.40.clone.1), kind=kCustom, calls=%fused_computation.160 | custom fusion | bytes 10628 | tf_op jit(solution)/shard_map/scatter | solution.py:167
  32.4 32.4 %all_gather.20 = bf16[128,512]{0,1:T(8,128)(2,1)S(1)} all-gather(bf16[128,64]{0,1:T(8,128)(2,1)S(1)} %convert_element_type.174), channel_id=1, replica_groups=mesh['shard'=4,'head'=4,'tensor'=2] {'shard','tensor'}, dimensions={1}, use_global_device_ids=true | all-gather | bytes 147456 | tf_op jit(solution)/shard_map/all_gather | solution.py:110
  64.8 30.9 %all_gather.19 = bf16[512,3,128]{2,0,1:T(8,128)(2,1)S(1)} all-gather(bf16[64,3,128]{2,0,1:T(8,128)(2,1)S(1)} %convert_element_type.169), channel_id=1, replica_groups=mesh['shard'=4,'head'=4,'tensor'=2] {'shard','tensor'}, dimensions={0}, use_global_device_ids=true | all-gather | bytes 442368 | tf_op jit(solution)/shard_map/all_gather | solution.py:109
  96.5 5.1 fusion.48
  107.7 3.5 multiply_reduce_fusion.1
  120.4 3.6 convolution_convert_fusion
  124.1 45.4 %fusion = bf16[1184,512]{1,0:T(8,128)(2,1)S(1)} fusion(bf16[4728,512]{1,0:T(8,128)(2,1)} %convolution_convert_fusion), kind=kCustom, calls=%all-reduce-scatter | all-reduce-scatter fusion | flops 2424833 | bytes 6054400
  174.0 7.3 concatenate.18
  185.3 8.9 gather_fusion
  194.1 4.6 broadcast_in_dim.26
  198.7 5.6 all-to-all-start
  206.0 5.5 mul.488
  211.6 7.1 mul.489
  225.1 8.9 gather_fusion.2
  234.0 91.2 %all-to-all-done = bf16[8,1,664,512]{3,2,1,0:T(8,128)(2,1)} async-done(((bf16[8,1,664,512]{3,2,1,0:T(8,128)(2,1)}), bf16[8,1,664,512]{3,2,1,0:T(8,128)(2,1)}, u32[]{:S(2)}, u32[]{:S(2)}) %all-to-all-start) | async-done | bytes 5439520 | tf_op jit(solution)/shard_map/all_to_all | solution.py:63
  325.2 4.7 broadcast_in_dim.30
  329.9 4.8 all-to-all-start.2
  335.5 19.4 %all-gather.8.cloned.1.call-done = bf16[1,512,1024]{2,1,0:T(8,128)(2,1)} async-done(((bf16[1,128,1024]{2,1,0:T(8,128)(2,1)}), bf16[1,512,1024]{2,1,0:T(8,128)(2,1)}) %all-gather.8.cloned.1.call-update) | async-done | bytes 1048592 | tf_op jit(solution)/shard_map/all_gather | solution.py:117
  354.9 12.4 %fusion.31 = f32[4,2,664,1024]{3,2,1,0:T(8,128)} fusion(bf16[1,512,1024]{2,1,0:T(8,128)(2,1)} %all-gather.8.cloned.1.call-done, bf16[4,2,664,512]{3,2,1,0:T(8,128)(2,1)} %bitcast.240), kind=kOutput, calls=%fused_computation.48 | convolution fusion | flops 5570035712 | bytes 28246016 | tf_op jit(solution)/shard_map/stecd,edf->stecf/dot_general | solution.py:171
  367.4 88.5 %all-to-all-done.2 = bf16[8,1,664,512]{3,2,1,0:T(8,128)(2,1)} async-done(((bf16[8,1,664,512]{3,2,1,0:T(8,128)(2,1)}), bf16[8,1,664,512]{3,2,1,0:T(8,128)(2,1)}, u32[]{:S(2)}, u32[]{:S(2)}) %all-to-all-start.2) | async-done | bytes 5439520 | tf_op jit(solution)/shard_map/all_to_all | solution.py:63
  455.9 13.5 %fusion.65 = bf16[1,1024,512]{2,1,0:T(8,128)(2,1)S(1)} fusion(f32[4,2,664,1024]{3,2,1,0:T(8,128)} %fusion.31, bf16[4,2,664,512]{3,2,1,0:T(8,128)(2,1)} %bitcast.244), kind=kOutput, calls=%fused_computation.89 | convolution fusion | flops 5619515392 | bytes 28246016 | tf_op jit(solution)/shard_map/stecf,stecd->efd/dot_general | solution.py:191
  472.8 23.0 %reduce-scatter.18.cloned.1.call-done = bf16[128,1024]{1,0:T(8,128)(2,1)} async-done(((bf16[512,1024]{1,0:T(8,128)(2,1)}), bf16[128,1024]{1,0:T(8,128)(2,1)}) %reduce-scatter.18.cloned.1.call-update) | async-done | bytes 262160
  500.1 17.0 %all-gather.10.cloned.1.call-done = bf16[1,1024,512]{2,1,0:T(8,128)(2,1)} async-done(((bf16[1,1024,128]{2,1,0:T(8,128)(2,1)}), bf16[1,1024,512]{2,1,0:T(8,128)(2,1)}) %all-gather.10.cloned.1.call-update) | async-done | bytes 1048592 | tf_op jit(solution)/shard_map/all_gather | solution.py:118
  517.1 14.0 %fusion.40 = bf16[4,2,664,512]{3,2,1,0:T(8,128)(2,1)} fusion(f32[4,2,664,1024]{3,2,1,0:T(8,128)} %fusion.31, bf16[1,1024,512]{2,1,0:T(8,128)(2,1)} %all-gather.10.cloned.1.call-done), kind=kOutput, calls=%fused_computation.62 | convolution fusion | flops 5621710848 | bytes 28246016 | tf_op jit(solution)/shard_map/stecf,efd->stecd/dot_general | solution.py:173
  531.0 6.2 all-to-all-start.1
  537.2 21.8 %fusion.9 = bf16[4,2,1,664,1024]{4,3,1,0,2:T(8,128)(2,1)S(1)} fusion(f32[4,2,664,1024]{3,2,1,0:T(8,128)} %fusion.31, bf16[1,1024,512]{2,1,0:T(8,128)(2,1)S(1)} %copy-done.78, bf16[4,2,664,512]{3,2,1,0:T(8,128)(2,1)} %bitcast.236), kind=kOutput, calls=%fused_computation.15 | convolution fusion | flops 5678825472 | bytes 39124992 | tf_op jit(solution)/shard_map/stecd,efd->stecf/dot_general | solution.py:194
  559.1 4.1 copy-done.79
  563.2 7.8 fusion.43
  571.0 86.5 %all-to-all-done.1 = bf16[8,1,664,512]{3,2,1,0:T(8,128)(2,1)} async-done(((bf16[8,1,664,512]{3,2,1,0:T(8,128)(2,1)}), bf16[8,1,664,512]{3,2,1,0:T(8,128)(2,1)}, u32[]{:S(2)}, u32[]{:S(2)}) %all-to-all-start.1) | async-done | bytes 5439520 | tf_op jit(solution)/shard_map/all_to_all | solution.py:71
  657.5 4.8 all-to-all-start.3
  662.4 6.4 convert_reduce_fusion.1
  668.8 113.0 %all-to-all-done.3 = bf16[8,1,664,512]{3,2,1,0:T(8,128)(2,1)} async-done(((bf16[8,1,664,512]{3,2,1,0:T(8,128)(2,1)}), bf16[8,1,664,512]{3,2,1,0:T(8,128)(2,1)}, u32[]{:S(2)}, u32[]{:S(2)}) %all-to-all-start.3) | async-done | bytes 5439520 | tf_op jit(solution)/shard_map/all_to_all | solution.py:71
  781.8 4.3 convert_reduce_fusion
  786.1 2.9 concatenate.17
  789.0 11.3 gather_fusion.3
  800.3 6.9 reshape.414
  807.2 9.8 reduce_sum.227
  817.0 5.5 concatenate.15
  822.5 11.1 gather_fusion.1
  833.6 7.0 reshape.405
  840.7 16.8 %multiply_reduce_fusion.2 = (f32[1182,2]{1,0:T(8,128)}, f32[1182,512]{1,0:T(8,128)}) fusion(f32[1182,2,512]{2,1,0:T(2,128)} %reshape.405, f32[1182,512]{1,0:T(8,128)} %copy-done.3, f32[1182,2]{1,0:T(8,128)S(1)} %copy-done.19), kind=kLoop, calls=%fused_computation.55 | loop fusion | flops 4233924 | bytes 9701856 | tf_op jit(solution)/shard_map/reduce_sum | solution.py:187
  859.0 4.0 multiply_reduce_fusion.7
  863.1 3.0 convert_bitcast_fusion
  866.1 12.7 %fusion.60 = bf16[1,512,1024]{2,1,0:T(8,128)(2,1)} fusion(bf16[4,2,1,664,1024]{4,3,1,0,2:T(8,128)(2,1)} %copy-done.79, bf16[4,2,664,512]{3,2,1,0:T(8,128)(2,1)} %bitcast.242), kind=kOutput, calls=%fused_computation.88 | convolution fusion | flops 5570560000 | bytes 17367040 | tf_op jit(solution)/shard_map/stecd,stecf->edf/dot_general | solution.py:198
  879.0 23.6 %all-gather.12.cloned.1.call-done = bf16[4,1182,512]{2,1,0:T(8,128)(2,1)} async-done(((bf16[1,1182,512]{2,1,0:T(8,128)(2,1)}), bf16[4,1182,512]{2,1,0:T(8,128)(2,1)}) %all-gather.12.cloned.1.call-update) | async-done | bytes 4841488 | tf_op jit(solution)/shard_map/all_gather | solution.py:221
  902.6 5.7 reshape.467
  908.3 3.9 convolution_convert_fusion.1
  914.8 4.9 copy.137
  919.7 6.0 convolution_convert_fusion.2
  925.7 7.5 multiply_reduce_fusion
  934.8 11.8 multiply_convert_fusion
  946.6 5.2 multiply_convert_fusion.3
  954.3 5.4 multiply_convert_fusion.2
  962.2 5.2 fusion.128
  967.6 6.8 fusion.70
  974.5 6.7 bitcast_convert_fusion
  988.8 39.8 %reduce-scatter.14.cloned.1.call-done = f32[128,64]{0,1:T(8,128)} async-done(((f32[128,512]{0,1:T(8,128)}), f32[128,64]{0,1:T(8,128)}) %reduce-scatter.14.cloned.1.call-update) | async-done | bytes 32784 | tf_op jit(solution)/shard_map/reduce_scatter | solution.py:279
  1030.0 64.1 %reduce-scatter.12.cloned.1.call-done = f32[64,3,128]{2,0,1:T(8,128)} async-done(((f32[512,3,128]{2,0,1:T(8,128)}), f32[64,3,128]{2,0,1:T(8,128)}) %reduce-scatter.12.cloned.1.call-update) | async-done | bytes 98320 | tf_op jit(solution)/shard_map/reduce_scatter | solution.py:278
  1095.8 49.4 %reduce-scatter.10.cloned.1.call-done = bf16[6,197,512]{2,1,0:T(8,128)(2,1)} async-done(((bf16[24,197,512]{2,1,0:T(8,128)(2,1)}), bf16[6,197,512]{2,1,0:T(8,128)(2,1)}) %reduce-scatter.10.cloned.1.call-update) | async-done | bytes 1210384 | tf_op jit(solution)/shard_map/reduce_scatter | solution.py:261
  1147.8 3.2 reshape.416
  1151.0 4.1 multiply_add_fusion
  1155.1 3.5 reshape.417
  1158.6 39.5 %all-reduce.6 = (f32[4,512]{1,0:T(4,128)S(1)}, f32[512,4]{0,1:T(4,128)S(1)}) all-reduce(f32[4,512]{1,0:T(4,128)S(1)} %pad_maximum_fusion.5, f32[512,4]{0,1:T(4,128)S(1)} %fusion.129), channel_id=1, replica_groups=mesh['shard'=4,'head'=4,'tensor'=2] {'shard','head','tensor'}, use_global_device_ids=true, to_apply=%region_29.30 | all-reduce | flops 4096 | bytes 32768 | tf_op jit(solution)/shard_map/psum | solution.py:276
  (261 shorter events, 74.8 us)
Async XLA Ops:
  7.2 7.3 copy-start.45
  7.2 7.4 copy-start.35
  7.2 7.4 copy-start.51
  7.2 88.6 %all-gather.6.cloned.1.call-start = ((), (), s32[]{:S(2)}) async-start(), calls=%async_computation.9 | async-start | bytes 6144000 | tf_op jit(solution)/shard_map/all_gather | solution.py:116
  8.9 6.9 copy-start.69
  11.6 172.0 %copy-start.67 = (f32[1,512]{1,0:T(1,128)}, f32[1,512]{1,0:T(1,128)S(1)}, u32[]{:S(2)}) copy-start(f32[1,512]{1,0:T(1,128)S(1)} %get-tuple-element.63) | copy-start | bytes 6148
  64.8 54.6 %copy-start.26 = (bf16[128,512]{0,1:T(8,128)(2,1)}, bf16[128,512]{0,1:T(8,128)(2,1)S(1)}, u32[]{:S(2)}) copy-start(bf16[128,512]{0,1:T(8,128)(2,1)S(1)} %all_gather.20) | copy-start | bytes 393220
  105.6 5.7 copy-start.15
  124.1 46.7 %copy-start.5 = (bf16[6,197,512]{2,1,0:T(8,128)(2,1)S(1)}, bf16[6,197,512]{2,1,0:T(8,128)(2,1)}, u32[]{:S(2)}) copy-start(bf16[6,197,512]{2,1,0:T(8,128)(2,1)} %param.22) | copy-start | bytes 3631108
  124.1 48.5 %copy-start.76 = (u32[32]{0:T(128)S(1)}, u32[32]{0:T(128)}, u32[]{:S(2)}) copy-start(u32[32]{0:T(128)} %constant.161) | copy-start | bytes 388
  169.4 4.5 collective-permute-start
  172.6 8.7 copy-start.7
  198.7 126.4 %all-to-all-start = ((bf16[8,1,664,512]{3,2,1,0:T(8,128)(2,1)}), bf16[8,1,664,512]{3,2,1,0:T(8,128)(2,1)}, u32[]{:S(2)}, u32[]{:S(2)}) async-start(bf16[8,1,664,512]{3,2,1,0:T(8,128)(2,1)} %bitcast.249), calls=%async_computation | async-start | bytes 10878976 | tf_op jit(solution)/shard_map/all_to_all | solution.py:63
  204.4 16.1 %copy-start.54 = (s32[1182,2]{0,1:T(2,128)}, s32[1182,2]{0,1:T(2,128)S(1)}, u32[]{:S(2)}) copy-start(s32[1182,2]{0,1:T(2,128)S(1)} %eq.24) | copy-start | bytes 28372
  206.0 12.6 %copy-start.3 = (f32[1182,512]{1,0:T(8,128)}, f32[1182,512]{1,0:T(8,128)S(1)}, u32[]{:S(2)}) copy-start(f32[1182,512]{1,0:T(8,128)S(1)} %reshape.421) | copy-start | bytes 7262212
  211.6 7.1 copy-start.56
  329.9 126.0 %all-to-all-start.2 = ((bf16[8,1,664,512]{3,2,1,0:T(8,128)(2,1)}), bf16[8,1,664,512]{3,2,1,0:T(8,128)(2,1)}, u32[]{:S(2)}, u32[]{:S(2)}) async-start(bf16[8,1,664,512]{3,2,1,0:T(8,128)(2,1)} %bitcast.250), calls=%async_computation.2 | async-start | bytes 10878976 | tf_op jit(solution)/shard_map/all_to_all | solution.py:63
  334.7 20.3 %all-gather.8.cloned.1.call-start = ((), (), s32[]{:S(2)}) async-start(), calls=%async_computation.10 | async-start | bytes 1310720 | tf_op jit(solution)/shard_map/all_gather | solution.py:117
  335.5 160.3 %reduce-scatter.18.cloned.1.call-start = ((), (), s32[]{:S(2)}) async-start(), calls=%async_computation.17 | async-start | bytes 1310720
  471.3 26.1 %copy-start.28 = (f32[1,1024,128]{2,1,0:T(8,128)S(1)}, f32[1,1024,128]{2,1,0:T(8,128)}, u32[]{:S(2)}) copy-start(f32[1,1024,128]{2,1,0:T(8,128)} %param.41) | copy-start | bytes 1572868
  471.4 26.1 %copy-start.29 = (f32[1,1024,128]{2,1,0:T(8,128)S(1)}, f32[1,1024,128]{2,1,0:T(8,128)}, u32[]{:S(2)}) copy-start(f32[1,1024,128]{2,1,0:T(8,128)} %param.42) | copy-start | bytes 1572868
  472.7 44.3 %all-gather.10.cloned.1.call-start = ((), (), s32[]{:S(2)}) async-start(), calls=%async_computation.11 | async-start | bytes 1310720 | tf_op jit(solution)/shard_map/all_gather | solution.py:118
  531.0 6.2 copy-start.78
  531.0 126.5 %all-to-all-start.1 = ((bf16[8,1,664,512]{3,2,1,0:T(8,128)(2,1)}), bf16[8,1,664,512]{3,2,1,0:T(8,128)(2,1)}, u32[]{:S(2)}, u32[]{:S(2)}) async-start(bf16[8,1,664,512]{3,2,1,0:T(8,128)(2,1)} %bitcast.266), calls=%async_computation.1 | async-start | bytes 10878976 | tf_op jit(solution)/shard_map/all_to_all | solution.py:71
  537.2 26.0 %copy-start.77 = (bf16[1,512,1024]{2,1,0:T(8,128)(2,1)S(1)}, bf16[1,512,1024]{2,1,0:T(8,128)(2,1)}, u32[]{:S(2)}) copy-start(bf16[1,512,1024]{2,1,0:T(8,128)(2,1)} %all-gather.8.cloned.1.call-done) | copy-start | bytes 3145732
  657.5 124.3 %all-to-all-start.3 = ((bf16[8,1,664,512]{3,2,1,0:T(8,128)(2,1)}), bf16[8,1,664,512]{3,2,1,0:T(8,128)(2,1)}, u32[]{:S(2)}, u32[]{:S(2)}) async-start(bf16[8,1,664,512]{3,2,1,0:T(8,128)(2,1)} %bitcast.265), calls=%async_computation.3 | async-start | bytes 10878976 | tf_op jit(solution)/shard_map/all_to_all | solution.py:71
  662.3 240.2 %all-gather.12.cloned.1.call-start = ((), (), s32[]{:S(2)}) async-start(), calls=%async_computation.16 | async-start | bytes 6062080 | tf_op jit(solution)/shard_map/all_gather | solution.py:221
  833.6 7.0 copy-start.19
  840.6 18.2 %copy-start.55 = (s32[1182,2]{0,1:T(2,128)S(1)}, s32[1182,2]{0,1:T(2,128)}, u32[]{:S(2)}) copy-start(s32[1182,2]{0,1:T(2,128)} %copy-done.54) | copy-start | bytes 28372
  840.6 18.2 %copy-start.32 = (f32[1182,4]{0,1:T(4,128)S(1)}, f32[1182,4]{0,1:T(4,128)}, u32[]{:S(2)}) copy-start(f32[1182,4]{0,1:T(4,128)} %copy-done.31) | copy-start | bytes 56740
  840.6 18.2 %copy-start.40 = (f32[1182]{0:T(1024)S(1)}, f32[1182]{0:T(1024)}, u32[]{:S(2)}) copy-start(f32[1182]{0:T(1024)} %copy-done.39) | copy-start | bytes 14188
  840.6 18.2 %copy-start.48 = (f32[1182]{0:T(1024)S(1)}, f32[1182]{0:T(1024)}, u32[]{:S(2)}) copy-start(f32[1182]{0:T(1024)} %copy-done.47) | copy-start | bytes 14188
  840.7 18.3 %copy-start.2 = (f32[1182,512]{1,0:T(8,128)S(1)}, f32[1182,512]{1,0:T(8,128)}, u32[]{:S(2)}) copy-start(f32[1182,512]{1,0:T(8,128)} %copy-done.1) | copy-start | bytes 7262212
  840.7 18.3 %copy-start.42 = (f32[1182]{0:T(1024)S(1)}, f32[1182]{0:T(1024)}, u32[]{:S(2)}) copy-start(f32[1182]{0:T(1024)} %copy-done.41) | copy-start | bytes 14188
  840.7 18.3 %copy-start.50 = (f32[1182]{0:T(1024)S(1)}, f32[1182]{0:T(1024)}, u32[]{:S(2)}) copy-start(f32[1182]{0:T(1024)} %copy-done.49) | copy-start | bytes 14188
  840.7 18.3 %copy-start.57 = (f32[512,4]{0,1:T(4,128)S(1)}, f32[512,4]{0,1:T(4,128)}, u32[]{:S(2)}) copy-start(f32[512,4]{0,1:T(4,128)} %param.35) | copy-start | bytes 24580
  840.7 18.3 %copy-start.68 = (f32[1,512]{1,0:T(1,128)S(1)}, f32[1,512]{1,0:T(1,128)}, u32[]{:S(2)}) copy-start(f32[1,512]{1,0:T(1,128)} %copy-done.67) | copy-start | bytes 6148
  866.1 117.1 %reduce-scatter.16.cloned.1.call-start = ((), (), s32[]{:S(2)}) async-start(), calls=%async_computation.15 | async-start | bytes 1310720 | tf_op jit(solution)/shard_map/reduce_scatter | solution.py:264
  878.9 29.4 %copy-start.27 = (bf16[128,512]{0,1:T(8,128)(2,1)S(1)}, bf16[128,512]{0,1:T(8,128)(2,1)}, u32[]{:S(2)}) copy-start(bf16[128,512]{0,1:T(8,128)(2,1)} %copy-done.26) | copy-start | bytes 393220
  878.9 149.7 %reduce-scatter.14.cloned.1.call-start = ((), (), s32[]{:S(2)}) async-start(), calls=%async_computation.14 | async-start | bytes 294912 | tf_op jit(solution)/shard_map/reduce_scatter | solution.py:279
  912.2 7.5 copy-start.25
  919.7 6.0 copy-start.14
  946.6 7.7 copy-start.16
  954.3 7.9 copy-start.12
  967.3 7.1 copy-start.34
  967.4 126.8 %reduce-scatter.12.cloned.1.call-start = ((), (), s32[]{:S(2)}) async-start(), calls=%async_computation.13 | async-start | bytes 884736 | tf_op jit(solution)/shard_map/reduce_scatter | solution.py:278
  974.4 170.8 %reduce-scatter.10.cloned.1.call-start = ((), (), s32[]{:S(2)}) async-start(), calls=%async_computation.12 | async-start | bytes 6144000 | tf_op jit(solution)/shard_map/reduce_scatter | solution.py:261
  981.8 6.8 copy-start.10
  981.8 46.8 %copy-start.46 = (f32[128,64]{0,1:T(8,128)S(1)}, f32[128,64]{0,1:T(8,128)}, u32[]{:S(2)}) copy-start(f32[128,64]{0,1:T(8,128)} %param.32) | copy-start | bytes 98308
  983.2 162.0 %copy-start.6 = (bf16[6,197,512]{2,1,0:T(8,128)(2,1)S(1)}, bf16[6,197,512]{2,1,0:T(8,128)(2,1)}, u32[]{:S(2)}) copy-start(bf16[6,197,512]{2,1,0:T(8,128)(2,1)} %param.22) | copy-start | bytes 3631108
  983.2 162.0 %copy-start.66 = (f32[1,512]{1,0:T(1,128)S(1)}, f32[1,512]{1,0:T(1,128)}, u32[]{:S(2)}) copy-start(f32[1,512]{1,0:T(1,128)} %copy-done.65) | copy-start | bytes 6148
  985.8 42.8 %copy-start.60 = (f32[128,64]{0,1:T(8,128)S(1)}, f32[128,64]{0,1:T(8,128)}, u32[]{:S(2)}) copy-start(f32[128,64]{0,1:T(8,128)} %param.33) | copy-start | bytes 98308
  985.8 42.8 %copy-start.61 = (f32[128,64]{0,1:T(8,128)S(1)}, f32[128,64]{0,1:T(8,128)}, u32[]{:S(2)}) copy-start(f32[128,64]{0,1:T(8,128)} %param.34) | copy-start | bytes 98308
  985.8 108.3 %copy-start.36 = (f32[64,3,128]{2,0,1:T(8,128)S(1)}, f32[64,3,128]{2,0,1:T(8,128)}, u32[]{:S(2)}) copy-start(f32[64,3,128]{2,0,1:T(8,128)} %param.29) | copy-start | bytes 294916
  985.8 108.3 %copy-start.52 = (f32[64,3,128]{2,0,1:T(8,128)S(1)}, f32[64,3,128]{2,0,1:T(8,128)}, u32[]{:S(2)}) copy-start(f32[64,3,128]{2,0,1:T(8,128)} %param.30) | copy-start | bytes 294916
  985.8 108.3 %copy-start.53 = (f32[64,3,128]{2,0,1:T(8,128)S(1)}, f32[64,3,128]{2,0,1:T(8,128)}, u32[]{:S(2)}) copy-start(f32[64,3,128]{2,0,1:T(8,128)} %param.31) | copy-start | bytes 294916
  988.8 162.2 %copy-start.63 = (f32[1182]{0:T(1024)S(1)}, f32[1182]{0:T(1024)}, u32[]{:S(2)}) copy-start(f32[1182]{0:T(1024)} %div.151) | copy-start | bytes 14188
  988.8 162.2 %copy-start.64 = (f32[1182]{0:T(1024)S(1)}, f32[1182]{0:T(1024)}, u32[]{:S(2)}) copy-start(f32[1182]{0:T(1024)} %rsqrt.22) | copy-start | bytes 14188
  1155.1 43.1 %copy-start.62 = (f32[4,512]{1,0:T(4,128)S(1)}, f32[4,512]{1,0:T(4,128)}, u32[]{:S(2)}) copy-start(f32[4,512]{1,0:T(4,128)} %param.26) | copy-start | bytes 24580
  1155.1 43.1 %copy-start.72 = (f32[4,512]{1,0:T(4,128)S(1)}, f32[4,512]{1,0:T(4,128)}, u32[]{:S(2)}) copy-start(f32[4,512]{1,0:T(4,128)} %param.27) | copy-start | bytes 24580
  1155.1 43.1 %copy-start.73 = (f32[4,512]{1,0:T(4,128)S(1)}, f32[4,512]{1,0:T(4,128)}, u32[]{:S(2)}) copy-start(f32[4,512]{1,0:T(4,128)} %param.28) | copy-start | bytes 24580
  1155.1 43.7 %copy-start.58 = (f32[512,4]{0,1:T(4,128)S(1)}, f32[512,4]{0,1:T(4,128)}, u32[]{:S(2)}) copy-start(f32[512,4]{0,1:T(4,128)} %param.35) | copy-start | bytes 24580
  1155.1 43.7 %copy-start.74 = (f32[512,4]{0,1:T(4,128)S(1)}, f32[512,4]{0,1:T(4,128)}, u32[]{:S(2)}) copy-start(f32[512,4]{0,1:T(4,128)} %param.36) | copy-start | bytes 24580
  1155.1 43.7 %copy-start.75 = (f32[512,4]{0,1:T(4,128)S(1)}, f32[512,4]{0,1:T(4,128)}, u32[]{:S(2)}) copy-start(f32[512,4]{0,1:T(4,128)} %param.37) | copy-start | bytes 24580
  (30 other events, 76.6 us)
Sparse Core Ops, SparseCore 0:
  14.7 41.2 all-gather.5
  337.7 17.2 all-gather.7
  472.9 22.8 reduce-scatter.17
  500.2 16.8 all-gather.9
  866.2 36.2 all-gather.11
  905.1 24.8 reduce-scatter.15
  967.5 61.0 reduce-scatter.13
  1031.9 62.1 reduce-scatter.11
  1096.9 48.2 reduce-scatter.9
where the time goes:
time: 1220 us; the launch traced here: 1210 us
  waiting for transfers between devices  616 us (50%)
  local copies, waits for them, and re-layouts  167 us (14%)
  matrix products  153 us (13%)
  blocking collectives  148 us (12%)
  other arithmetic  83.5 us (7%)
  starting transfers between devices  23.2 us (2%)
  between operations  16 us (1%)
    all_to_all x2, waiting for transfers between devices, return_rows(): lax.all_to_all(flat_rows.astype(jnp.bfloat16), ('shard', 'tensor'), split...  199 us
    all_to_all x2, waiting for transfers between devices, send_rows(): lax.all_to_all(flat_copies, ('shard', 'tensor'), split_axis=0, concat_axi...  180 us
    reduce_scatter x1, waiting for transfers between devices, on_device(): lax.psum_scatter(qkv_grad, ('shard', 'tensor'), scatter_dimension=0, tile...  64.1 us
    reduce_scatter x1, waiting for transfers between devices, on_device(): lax.psum_scatter(normed_part.astype(jnp.bfloat16), 'head', scatter_dimens...  49.4 us
    unnamed x1, blocking collectives  45.4 us
    reduce_scatter x1, waiting for transfers between devices, on_device(): lax.psum_scatter(attn_grad, ('shard', 'tensor'), scatter_dimension=1, til...  39.8 us
    psum x1, blocking collectives, on_device(): lax.psum((norm_grad, router_grad), ('shard', 'head', 'tensor'))  39.5 us
    all_gather x1, blocking collectives, on_device(): lax.all_gather(attn_weight.astype(jnp.bfloat16), ('shard', 'tensor'), axi...  32.4 us
  transfers between devices with their start and end apart: 14, of which 11 were waited for; matrix products, arithmetic and copies ran while one was open for 16% of the time, Pallas kernels for 0%

commit v1 on v0

--- a/solution.py
+++ b/solution.py
@@ -3,6 +3,8 @@
 import jax
 import jax.numpy as jnp
 from jax import lax
+from jax.experimental import pallas as pl
+from jax.experimental.pallas import tpu as pltpu
 from jax.sharding import PartitionSpec as P
 
 HEAD_DIM = 64
@@ -74,7 +76,7 @@
     return jnp.sum(arrived.reshape(partial_rows.shape), axis=1)
 
 
-def on_device(
+def slot_plan(
     block_input,
     cotangent,
     routes,
@@ -323,9 +325,746 @@
     )
 
 
+PAD = 208
+SLOT_PAD = 16
+
+
+def kernel_params(megabytes):
+    return pltpu.CompilerParams(vmem_limit_bytes=megabytes << 20)
+
+
+def cost(flops, moved):
+    return pl.CostEstimate(flops=int(flops), bytes_accessed=int(moved), transcendentals=0)
+
+
+def mm(left, right):
+    return lax.dot_general(left, right, (((1,), (0,)), ((), ())), preferred_element_type=jnp.float32)
+
+
+def mm_turned(left, right):
+    return lax.dot_general(left, right, (((1,), (1,)), ((), ())), preferred_element_type=jnp.float32)
+
+
+def mm_rows(left, right):
+    return lax.dot_general(left, right, (((0,), (0,)), ((), ())), preferred_element_type=jnp.float32)
+
+
+def unit_of(values):
+    center = jnp.mean(values, axis=-1, keepdims=True)
+    shifted = values - center
+    inverse = lax.rsqrt(jnp.mean(shifted * shifted, axis=-1, keepdims=True) + EPS_NORM)
+    return (shifted * inverse, inverse)
+
+
+def unit_backward(grad_rows, unit_rows, inverse, gain_row):
+    scaled = grad_rows * gain_row
+    inner_grad = (
+        scaled
+        - jnp.mean(scaled, axis=-1, keepdims=True)
+        - unit_rows * jnp.mean(scaled * unit_rows, axis=-1, keepdims=True)
+    )
+    return inner_grad * inverse
+
+
+def slot_kernel(experts, capacity, row_ref, column_ref, slot_row_ref, slot_column_ref):
+    none = 1 << 20
+    tokens = row_ref.shape[1]
+    lanes = lax.broadcasted_iota(jnp.int32, (PAD, 128), 1)
+    rows_of = lax.broadcasted_iota(jnp.int32, (8, tokens), 0)
+
+    def ranks(named, rank, expert):
+        return jnp.where(
+            named[0] == expert, rank[0], jnp.where(named[1] == expert, rank[1], none)
+        )
+
+    routes_row, ranks_row = (row_ref[0:1], row_ref[1:2]), (row_ref[2:3], row_ref[3:4])
+    all_rows = jnp.full((8, tokens), -1, jnp.int32)
+    row_of = [ranks(routes_row, ranks_row, e) for e in range(experts)]
+    totals = [jnp.zeros((1, tokens), jnp.float32) for e in range(experts)]
+    for block in range(tokens // PAD):
+        part = column_ref[block * PAD : (block + 1) * PAD]
+        routes_col, ranks_col = (part[:, 0:1], part[:, 1:2]), (part[:, 2:3], part[:, 3:4])
+        result = jnp.full((PAD, 128), -1, jnp.int32)
+        for e in range(experts):
+            column = ranks(routes_col, ranks_col, e)
+            totals[e] = totals[e] + jnp.sum(
+                jnp.where(column < row_of[e], 1.0, 0.0), axis=0, keepdims=True
+            )
+            before = jnp.sum(
+                jnp.where(row_of[e] < column, 1.0, 0.0), axis=1, keepdims=True
+            ).astype(jnp.int32)
+            slot = jnp.where((column < none) & (before < capacity), before, -1)
+            result = jnp.where(lanes == e, slot, result)
+        slot_column_ref[block * PAD : (block + 1) * PAD] = result
+    for e in range(experts):
+        before = totals[e].astype(jnp.int32)
+        slot = jnp.where((row_of[e] < none) & (before < capacity), before, -1)
+        all_rows = jnp.where(rows_of == e, slot, all_rows)
+    slot_row_ref[...] = all_rows
+
+
+def find_slots(routes, priority, experts, capacity):
+    images, length, _ = routes.shape
+    tokens = images * PAD
+    table = jnp.concatenate([routes, priority.reshape(images, length, 2)], axis=2)
+    table = jnp.pad(table, ((0, 0), (0, PAD - length), (0, 0)), constant_values=-1)
+    table = table.reshape(tokens, 4)
+    columns = jnp.pad(table, ((0, 0), (0, 4)))
+    return pl.pallas_call(
+        partial(slot_kernel, experts, capacity),
+        out_shape=(
+            jax.ShapeDtypeStruct((8, tokens), jnp.int32),
+            jax.ShapeDtypeStruct((tokens, 128), jnp.int32),
+        ),
+        compiler_params=kernel_params(32),
+        cost_estimate=cost(1e10, 1e6),
+        name="find_slots",
+    )(columns.T, columns)
+
+
+def dense_kernel(place_ref, pieces_ref, full_ref, sems):
+    count, kinds, rows, columns = pieces_ref.shape
+    across = full_ref.shape[2] // columns
+    copies = []
+    for piece in range(count):
+        down, over = piece // across, piece % across
+        copies.append(
+            pltpu.make_async_copy(
+                pieces_ref.at[place_ref[piece]],
+                full_ref.at[:, down * rows : (down + 1) * rows, over * columns : (over + 1) * columns],
+                sems.at[piece],
+            )
+        )
+    for copy in copies:
+        copy.start()
+    for copy in copies:
+        copy.wait()
+
+
+def join_dense(places, pieces, model_width):
+    count, kinds = pieces.shape[:2]
+    return pl.pallas_call(
+        dense_kernel,
+        out_shape=jax.ShapeDtypeStruct((kinds, model_width, model_width), pieces.dtype),
+        in_specs=[pl.BlockSpec(memory_space=pltpu.SMEM), pl.BlockSpec(memory_space=pl.ANY)],
+        out_specs=pl.BlockSpec(memory_space=pltpu.VMEM),
+        scratch_shapes=[pltpu.SemaphoreType.DMA((count,))],
+        compiler_params=kernel_params(16),
+        cost_estimate=cost(1e6, 4e6),
+        name="join_dense",
+    )(places, pieces)
+
+
+def attend_kernel(
+    length, experts, input_ref, norm_ref, dense_ref, router_ref,
+    normed_ref, projected_ref, probs_ref, context_ref, hidden_ref, second_ref, route_ref,
+):
+    low = jnp.bfloat16
+    values = input_ref[0].astype(jnp.float32)
+    width = values.shape[1]
+    unit, _ = unit_of(values)
+    normed = (unit * norm_ref[0:1] + norm_ref[1:2]).astype(low)
+    normed_ref[0] = normed
+    queries, key_rows, value_rows = (mm(normed, dense_ref[c]).astype(low) for c in range(3))
+    projected_ref[0, 0] = queries
+    projected_ref[0, 1] = key_rows
+    projected_ref[0, 2] = value_rows
+    first_half = lax.broadcasted_iota(jnp.int32, (PAD, 2 * HEAD_DIM), 1) < HEAD_DIM
+    is_key = lax.broadcasted_iota(jnp.int32, (PAD, PAD), 1) < length
+    zero = jnp.zeros((PAD, 2 * HEAD_DIM), low)
+    pairs = []
+    for pair in range(width // (2 * HEAD_DIM)):
+        at = slice(pair * 2 * HEAD_DIM, (pair + 1) * 2 * HEAD_DIM)
+        query, key, value = queries[:, at], key_rows[:, at], value_rows[:, at]
+        halves = []
+        for side in range(2):
+            mine = jnp.where(first_half == (side == 0), query, zero)
+            scores = mm_turned(mine, key) * (HEAD_DIM ** (-0.5))
+            scores = jnp.where(is_key, scores, -1e30)
+            top = jnp.max(scores, axis=-1, keepdims=True)
+            raised = jnp.exp(scores - top)
+            probs = (raised / jnp.sum(raised, axis=-1, keepdims=True)).astype(low)
+            probs_ref[0, 2 * pair + side] = probs
+            halves.append(mm(probs, value))
+        pairs.append(jnp.where(first_half, halves[0], halves[1]).astype(low))
+    context = jnp.concatenate(pairs, axis=1)
+    context_ref[0] = context
+    hidden = values + mm_turned(context, dense_ref[3])
+    hidden_ref[0] = hidden
+    unit, _ = unit_of(hidden)
+    second = (unit * norm_ref[2:3] + norm_ref[3:4]).astype(low)
+    second_ref[0] = second
+    logits = mm(second, router_ref[...])
+    is_expert = lax.broadcasted_iota(jnp.int32, logits.shape, 1) < experts
+    logits = jnp.where(is_expert, logits, -1e30)
+    raised = jnp.exp(logits - jnp.max(logits, axis=-1, keepdims=True))
+    route_ref[0] = raised / jnp.sum(raised, axis=-1, keepdims=True)
+
+
+def attend(length, experts, padded, norm_params, dense, router_wide):
+    images, _, width = padded.shape
+    heads = width // HEAD_DIM
+    low, wide = jnp.bfloat16, jnp.float32
+
+    def per_image(*shape):
+        return pl.BlockSpec((1,) + shape, lambda i: (i,) + (0,) * len(shape))
+
+    def whole(array):
+        return pl.BlockSpec(array.shape, lambda i: (0,) * array.ndim)
+
+    shapes = [
+        ((PAD, width), low), ((3, PAD, width), low), ((heads, PAD, PAD), low), ((PAD, width), low),
+        ((PAD, width), wide), ((PAD, width), low), ((PAD, 128), wide),
+    ]
+    return pl.pallas_call(
+        partial(attend_kernel, length, experts),
+        grid=(images,),
+        in_specs=[per_image(PAD, width), whole(norm_params), whole(dense), whole(router_wide)],
+        out_specs=[per_image(*s) for s, _ in shapes],
+        out_shape=[jax.ShapeDtypeStruct((images,) + s, t) for s, t in shapes],
+        compiler_params=kernel_params(48),
+        cost_estimate=cost(images * 2.5e9, images * 5e6),
+        name="attend",
+    )(padded, norm_params, dense, router_wide)
+
+
+def dispatch_kernel(slot_ref, second_ref, upstream_ref, route_ref, x_ref, g_ref, xt_ref, gt_ref):
+    low = jnp.bfloat16
+    expert = pl.program_id(0)
+    slots, tokens = x_ref.shape[1], second_ref.shape[0]
+    rows_of = lax.broadcasted_iota(jnp.int32, (8, tokens), 0)
+    slot_row = jnp.max(jnp.where(rows_of == expert, slot_ref[...], -1), axis=0, keepdims=True)
+    hot = lax.broadcasted_iota(jnp.int32, (slots, tokens), 0) == slot_row
+    hot = jnp.where(hot, 1.0, 0.0).astype(low)
+    lanes = lax.broadcasted_iota(jnp.int32, (tokens, 128), 1)
+    gate = jnp.sum(jnp.where(lanes == expert, route_ref[...], 0.0), axis=1, keepdims=True)
+    pair_grad = (gate * upstream_ref[...].astype(jnp.float32)).astype(low)
+    rows = mm(hot, second_ref[...]).astype(low)
+    x_ref[0] = rows
+    xt_ref[0] = rows.T
+    rows = mm(hot, pair_grad).astype(low)
+    g_ref[0] = rows
+    gt_ref[0] = rows.T
+
+
+def dispatch(slot_row, second, upstream, route_probs, experts, slots):
+    tokens, width = second.shape
+
+    def whole(array):
+        return pl.BlockSpec(array.shape, lambda e: (0,) * array.ndim)
+
+    flat = pl.BlockSpec((1, slots, width), lambda e: (e, 0, 0))
+    turned = pl.BlockSpec((1, width, slots), lambda e: (e, 0, 0))
+    low = jnp.bfloat16
+    return pl.pallas_call(
+        dispatch_kernel,
+        grid=(experts,),
+        in_specs=[whole(a) for a in (slot_row, second, upstream, route_probs)],
+        out_specs=[flat, flat, turned, turned],
+        out_shape=[jax.ShapeDtypeStruct((experts, slots, width), low)] * 2
+        + [jax.ShapeDtypeStruct((experts, width, slots), low)] * 2,
+        compiler_params=kernel_params(48),
+        cost_estimate=cost(4 * slots * tokens * width * experts, 1e7),
+        name="dispatch",
+    )(slot_row, second, upstream, route_probs)
+
+
+def expert_kernel(first, last, place_ref, x_ref, g_ref, xt_ref, gt_ref, *refs):
+    low = jnp.bfloat16
+    if first:
+        weights_ref, made_ref, back_ref, grads_ref = refs[:4]
+        rest = refs[4:]
+    else:
+        made_in, back_in, weights_ref, made_ref, back_ref, grads_ref = refs[:6]
+        rest = refs[6:]
+    held, sent, made_sum, back_sum, in_sems, out_sems = rest
+    expert, experts = pl.program_id(0), pl.num_programs(0)
+    parts = place_ref.shape[1]
+    _, kinds, rows, columns = weights_ref.shape
+    down = held.shape[2] // rows
+
+    def window(ref, slot, part):
+        tensor, head = part // down, part % down
+        return ref.at[
+            slot, :, head * rows : (head + 1) * rows, tensor * columns : (tensor + 1) * columns
+        ]
+
+    def fetch(which, slot, part):
+        return pltpu.make_async_copy(
+            weights_ref.at[place_ref[which, part]], window(held, slot, part), in_sems.at[slot, part]
+        )
+
+    def put(which, slot, part):
+        return pltpu.make_async_copy(
+            window(sent, slot, part), grads_ref.at[place_ref[which, part]], out_sems.at[slot, part]
+        )
+
+    slot = lax.rem(expert, 2)
+
+    @pl.when(expert == 0)
+    def _():
+        for part in range(parts):
+            fetch(0, 0, part).start()
+
+    @pl.when(expert + 1 < experts)
+    def _():
+        for part in range(parts):
+            fetch(expert + 1, 1 - slot, part).start()
+
+    for part in range(parts):
+        fetch(expert, slot, part).wait()
+
+    @pl.when(expert >= 2)
+    def _():
+        for part in range(parts):
+            put(expert - 2, slot, part).wait()
+
+    x, g, xt, gt = x_ref[0], g_ref[0], xt_ref[0], gt_ref[0]
+    units = held.shape[3]
+    tile = 256
+    for unit in range(0, units, tile):
+        at = slice(unit, unit + tile)
+        w_in, w_out = held[slot, 0, :, at], held[slot, 1, :, at]
+        v = mm(x, w_in)
+        grad = mm(g, w_out)
+        square = v * v
+        tanh = jnp.tanh(v * (0.7978845608028654 + 0.035677408136300125 * square))
+        half = 0.5 + 0.5 * tanh
+        active = (v * half).astype(low)
+        slope = half + v * (half * (1.0 - tanh)) * (
+            0.7978845608028654 + 0.10703222440890037 * square
+        )
+        pre_grad = (grad * slope).astype(low)
+        made = mm_turned(active, w_out)
+        back = mm_turned(pre_grad, w_in)
+        if unit == 0:
+            made_sum[...] = made
+            back_sum[...] = back
+        else:
+            made_sum[...] += made
+            back_sum[...] += back
+        sent[slot, 0, :, at] = mm(xt, pre_grad).astype(low)
+        sent[slot, 1, :, at] = mm(gt, active).astype(low)
+    made, back = made_sum[...], back_sum[...]
+    if not first:
+        made, back = made + made_in[0], back + back_in[0]
+    made_ref[0] = made.astype(made_ref.dtype)
+    back_ref[0] = back.astype(back_ref.dtype)
+    for part in range(parts):
+        put(expert, slot, part).start()
+
+    @pl.when(expert == experts - 1)
+    def _():
+        for part in range(parts):
+            put(expert - 1, 1 - slot, part).wait()
+        for part in range(parts):
+            put(expert, slot, part).wait()
+
+
+def run_experts(places, x, g, xt, gt, sums, weights, last):
+    experts, slots, width = x.shape
+    pieces, kinds, rows, columns = weights.shape
+    parts = places.shape[1]
+    units = parts * rows * columns // width
+    low = jnp.bfloat16
+    flat = pl.BlockSpec((1, slots, width), lambda e: (e, 0, 0))
+    turned = pl.BlockSpec((1, width, slots), lambda e: (e, 0, 0))
+    anywhere = pl.BlockSpec(memory_space=pl.ANY)
+    kept = low if last else jnp.float32
+    first = sums is None
+    given = () if first else tuple(sums)
+    return pl.pallas_call(
+        partial(expert_kernel, first, last),
+        grid=(experts,),
+        in_specs=[pl.BlockSpec(memory_space=pltpu.SMEM), flat, flat, turned, turned]
+        + [flat] * len(given)
+        + [anywhere],
+        out_specs=[flat, flat, anywhere],
+        out_shape=[jax.ShapeDtypeStruct((experts, slots, width), kept)] * 2
+        + [jax.ShapeDtypeStruct(weights.shape, low)],
+        scratch_shapes=[
+            pltpu.VMEM((2, kinds, width, units), low),
+            pltpu.VMEM((2, kinds, width, units), low),
+            pltpu.VMEM((slots, width), jnp.float32),
+            pltpu.VMEM((slots, width), jnp.float32),
+            pltpu.SemaphoreType.DMA((2, parts)),
+            pltpu.SemaphoreType.DMA((2, parts)),
+        ],
+        compiler_params=kernel_params(56),
+        cost_estimate=cost(12 * experts * slots * width * units, 3e7),
+        name="experts",
+    )(places, x, g, xt, gt, *given, weights)
+
+
+def combine_kernel(
+    experts, slot_ref, made_ref, back_ref, hidden_ref, upstream_ref, second_ref, route_ref,
+    norm_ref, router_ref, output_ref, grad_ref, router_grad_ref, norm_grad_ref,
+):
+    low = jnp.bfloat16
+    image = pl.program_id(0)
+    hidden = hidden_ref[0]
+    upstream = upstream_ref[0].astype(jnp.float32)
+    route_probs = route_ref[0]
+    slots = made_ref.shape[1]
+    lanes = lax.broadcasted_iota(jnp.int32, (PAD, slots), 1)
+    wide_lanes = lax.broadcasted_iota(jnp.int32, (PAD, 128), 1)
+    total = hidden
+    second_grad = jnp.zeros_like(hidden)
+    prob_sum = jnp.zeros((PAD, 128), jnp.float32)
+    for e in range(experts):
+        hot = jnp.where(lanes == slot_ref[0][:, e : e + 1], 1.0, 0.0).astype(low)
+        made = mm(hot, made_ref[e])
+        second_grad = second_grad + mm(hot, back_ref[e])
+        total = total + route_probs[:, e : e + 1] * made
+        gate_grad = jnp.sum(upstream * made, axis=-1, keepdims=True)
+        prob_sum = jnp.where(wide_lanes == e, gate_grad, prob_sum)
+    length = output_ref.shape[1]
+    output_ref[0] = total.astype(low)[:length]
+    inner = jnp.sum(route_probs * prob_sum, axis=-1, keepdims=True)
+    logit_grad = (route_probs * (prob_sum - inner)).astype(low)
+    second_grad = second_grad + mm_turned(logit_grad, router_ref[...])
+    unit, inverse = unit_of(hidden)
+    grad_ref[0] = upstream + unit_backward(second_grad, unit, inverse, norm_ref[2:3])
+    router_grad = mm_rows(logit_grad, second_ref[0])[:8]
+    gain = jnp.sum(second_grad * unit, axis=0, keepdims=True)
+    bias = jnp.sum(second_grad, axis=0, keepdims=True)
+    rows_of = lax.broadcasted_iota(jnp.int32, (8, hidden.shape[1]), 0)
+    norm_grad = jnp.where(rows_of == 2, gain, jnp.where(rows_of == 3, bias, 0.0))
+
+    @pl.when(image == 0)
+    def _():
+        router_grad_ref[...] = router_grad
+        norm_grad_ref[...] = norm_grad
+
+    @pl.when(image > 0)
+    def _():
+        router_grad_ref[...] += router_grad
+        norm_grad_ref[...] += norm_grad
+
+
+def combine(length, experts, slot_column, made, back, hidden, upstream, second, route_probs, norm_params, router_wide):
+    images, _, width = hidden.shape
+    low, wide = jnp.bfloat16, jnp.float32
+
+    def per_image(*shape):
+        return pl.BlockSpec((1,) + shape, lambda i: (i,) + (0,) * len(shape))
+
+    def whole(array):
+        return pl.BlockSpec(array.shape, lambda i: (0,) * array.ndim)
+
+    small = pl.BlockSpec((8, width), lambda i: (0, 0))
+    return pl.pallas_call(
+        partial(combine_kernel, experts),
+        grid=(images,),
+        in_specs=[
+            per_image(PAD, 128), whole(made), whole(back), per_image(PAD, width), per_image(PAD, width),
+            per_image(PAD, width), per_image(PAD, 128), whole(norm_params), whole(router_wide),
+        ],
+        out_specs=[per_image(length, width), per_image(PAD, width), small, small],
+        out_shape=[
+            jax.ShapeDtypeStruct((images, length, width), low),
+            jax.ShapeDtypeStruct((images, PAD, width), wide),
+            jax.ShapeDtypeStruct((8, width), wide),
+            jax.ShapeDtypeStruct((8, width), wide),
+        ],
+        compiler_params=kernel_params(48),
+        cost_estimate=cost(4 * images * PAD * experts * made.shape[1] * width, 2e7),
+        name="combine",
+    )(slot_column, made, back, hidden, upstream, second, route_probs, norm_params, router_wide)
+
+
+def attend_back_kernel(
+    place_ref, input_ref, norm_ref, dense_ref, normed_ref, projected_ref, probs_ref, context_ref, grad_ref,
+    input_grad_ref, norm_grad_ref, pieces_ref, sums, low_sums, sems,
+):
+    low = jnp.bfloat16
+    image, images = pl.program_id(0), pl.num_programs(0)
+
+    @pl.when(image == 0)
+    def _():
+        sums[...] = jnp.zeros_like(sums)
+        norm_grad_ref[...] = jnp.zeros_like(norm_grad_ref)
+
+    hidden_grad = grad_ref[0]
+    width = hidden_grad.shape[1]
+    attended_low = hidden_grad.astype(low)
+    context_grad = mm(attended_low, dense_ref[3]).astype(low)
+    sums[3] += mm_rows(attended_low, context_ref[0])
+    queries, key_rows, value_rows = projected_ref[0, 0], projected_ref[0, 1], projected_ref[0, 2]
+    first_half = lax.broadcasted_iota(jnp.int32, (PAD, 2 * HEAD_DIM), 1) < HEAD_DIM
+    zero = jnp.zeros((PAD, 2 * HEAD_DIM), low)
+    scale = HEAD_DIM ** (-0.5)
+    parts = [[], [], []]
+    for pair in range(width // (2 * HEAD_DIM)):
+        at = slice(pair * 2 * HEAD_DIM, (pair + 1) * 2 * HEAD_DIM)
+        query, key, value, grad = queries[:, at], key_rows[:, at], value_rows[:, at], context_grad[:, at]
+        halves = []
+        for side in range(2):
+            mine = jnp.where(first_half == (side == 0), grad, zero)
+            probs = probs_ref[0, 2 * pair + side]
+            wide = probs.astype(jnp.float32)
+            prob_grad = mm_turned(mine, value)
+            weighted = wide * prob_grad
+            score_grad = (
+                weighted - wide * jnp.sum(weighted, axis=-1, keepdims=True)
+            ).astype(low)
+            halves.append(
+                (mm(score_grad, key) * scale, mm_rows(score_grad, query) * scale, mm_rows(probs, grad))
+            )
+        for kind in range(3):
+            parts[kind].append(jnp.where(first_half, halves[0][kind], halves[1][kind]).astype(low))
+    normed = normed_ref[0]
+    normed_grad = None
+    for kind in range(3):
+        projected_grad = jnp.concatenate(parts[kind], axis=1)
+        sums[kind] += mm_rows(normed, projected_grad)
+        part = mm_turned(projected_grad, dense_ref[kind])
+        normed_grad = part if normed_grad is None else normed_grad + part
+    unit, inverse = unit_of(input_ref[0].astype(jnp.float32))
+    length = input_grad_ref.shape[1]
+    input_grad = hidden_grad + unit_backward(normed_grad, unit, inverse, norm_ref[0:1])
+    input_grad_ref[0] = input_grad[:length]
+    gain = jnp.sum(normed_grad * unit, axis=0, keepdims=True)
+    bias = jnp.sum(normed_grad, axis=0, keepdims=True)
+    rows_of = lax.broadcasted_iota(jnp.int32, (8, width), 0)
+    norm_grad_ref[...] += jnp.where(rows_of == 0, gain, jnp.where(rows_of == 1, bias, 0.0))
+
+    @pl.when(image == images - 1)
+    def _():
+        count, kinds, rows, columns = pieces_ref.shape
+        across = width // columns
+        low_sums[...] = sums[...].astype(low)
+        copies = []
+        for piece in range(count):
+            down, over = piece // across, piece % across
+            copies.append(
+                pltpu.make_async_copy(
+                    low_sums.at[:, down * rows : (down + 1) * rows, over * columns : (over + 1) * columns],
+                    pieces_ref.at[place_ref[piece]],
+                    sems.at[piece],
+                )
+            )
+        for copy in copies:
+            copy.start()
+        for copy in copies:
+            copy.wait()
+
+
+def attend_back(length, places, padded, norm_params, dense, normed, projected, probs, context, hidden_grad, pieces_shape):
+    images, _, width = padded.shape
+    heads = width // HEAD_DIM
+    low, wide = jnp.bfloat16, jnp.float32
+
+    def per_image(*shape):
+        return pl.BlockSpec((1,) + shape, lambda i: (i,) + (0,) * len(shape))
+
+    def whole(array):
+        return pl.BlockSpec(array.shape, lambda i: (0,) * array.ndim)
+
+    return pl.pallas_call(
+        attend_back_kernel,
+        grid=(images,),
+        in_specs=[
+            pl.BlockSpec(memory_space=pltpu.SMEM), per_image(PAD, width), whole(norm_params), whole(dense),
+            per_image(PAD, width), per_image(3, PAD, width), per_image(heads, PAD, PAD),
+            per_image(PAD, width), per_image(PAD, width),
+        ],
+        out_specs=[
+            per_image(length, width), pl.BlockSpec((8, width), lambda i: (0, 0)),
+            pl.BlockSpec(memory_space=pl.ANY),
+        ],
+        out_shape=[
+            jax.ShapeDtypeStruct((images, length, width), wide),
+            jax.ShapeDtypeStruct((8, width), wide),
+            jax.ShapeDtypeStruct(pieces_shape, low),
+        ],
+        scratch_shapes=[
+            pltpu.VMEM((4, width, width), wide),
+            pltpu.VMEM((4, width, width), low),
+            pltpu.SemaphoreType.DMA((pieces_shape[0],)),
+        ],
+        compiler_params=kernel_params(56),
+        cost_estimate=cost(images * 5e9, images * 6e6),
+        name="attend_back",
+    )(places, padded, norm_params, dense, normed, projected, probs, context, hidden_grad)
+
+
+def relay(block, axis, mask):
+    size = lax.axis_size(axis)
+    return lax.ppermute(block, axis, [(i, i ^ mask) for i in range(size)])
+
+
+def spread(block, stages):
+    pieces = block[None]
+    for axis, mask in stages:
+        pieces = jnp.concatenate([pieces, relay(pieces, axis, mask)], axis=0)
+    return pieces
+
+
+def collect(pieces, stages):
+    for axis, mask in reversed(stages):
+        half = pieces.shape[0] // 2
+        arrived = relay(pieces[half:], axis, mask)
+        total = pieces[:half].astype(jnp.float32) + arrived.astype(jnp.float32)
+        pieces = total.astype(pieces.dtype)
+    return pieces[0]
+
+
+def sum_all(value, stages):
+    for axis, mask in stages:
+        value = value + relay(value, axis, mask)
+    return value
+
+
+def mesh_stages(order):
+    def of(axis):
+        return [(axis, 1 << b) for b in range((lax.axis_size(axis) - 1).bit_length())]
+
+    by_name = {"z": of("shard"), "x": of("head")[1:], "y": of("tensor"), "core": of("head")[:1]}
+    return [stage for name in order for stage in by_name[name]]
+
+
+def relative_places(stages):
+    axes = ("shard", "tensor", "head")
+    shape = tuple(lax.axis_size(a) for a in axes)
+    place = jnp.zeros(shape, jnp.int32)
+    for bit, (axis, mask) in enumerate(stages):
+        apart = lax.broadcasted_iota(jnp.int32, shape, axes.index(axis)) ^ lax.axis_index(axis)
+        place = place + jnp.where((apart & mask) != 0, 1 << bit, 0)
+    return place
+
+
+def local_plan(
+    block_input,
+    cotangent,
+    routes,
+    priority,
+    norm_params,
+    norm_moment,
+    norm_square,
+    qkv_weight,
+    qkv_moment,
+    qkv_square,
+    attn_weight,
+    attn_moment,
+    attn_square,
+    router_weight,
+    router_moment,
+    router_square,
+    expert_in,
+    in_moment,
+    in_square,
+    expert_out,
+    out_moment,
+    out_square,
+):
+    images, length, model_width = block_input.shape
+    experts = lax.axis_size("shard")
+    capacity = 9 * images * length // (4 * experts)
+    slots = -(-capacity // SLOT_PAD) * SLOT_PAD
+    low = jnp.bfloat16
+    orders = [("z", "x", "y", "core"), ("z", "y", "x", "core")]
+    dense_stages = mesh_stages(orders[0])
+    dense_places = relative_places(dense_stages).reshape(-1)
+    dense_low = jnp.concatenate(
+        [qkv_weight.transpose(1, 0, 2), attn_weight.T[None]], axis=0
+    ).astype(low)
+    dense_pieces = spread(dense_low, dense_stages)
+    expert_low = jnp.stack([expert_in[0], expert_out[0].T]).astype(low)
+    parts = len(orders)
+    cut = expert_low.shape[2] // parts
+    expert_stages = [mesh_stages(o) for o in orders]
+    expert_places = [relative_places(s).reshape(experts, -1) for s in expert_stages]
+    expert_pieces = [
+        spread(expert_low[:, :, i * cut : (i + 1) * cut], s) for i, s in enumerate(expert_stages)
+    ]
+    router_wide = jnp.pad(router_weight, ((0, 0), (0, 128 - experts))).astype(low)
+    slot_row, slot_column = find_slots(routes, priority, experts, capacity)
+    slot_column = slot_column.reshape(images, PAD, 128)
+    fill = ((0, 0), (0, PAD - length), (0, 0))
+    padded, upstream = jnp.pad(block_input, fill), jnp.pad(cotangent, fill)
+    dense = join_dense(dense_places, dense_pieces, model_width)
+    normed, projected, probs, context, hidden, second, route_probs = attend(
+        length, experts, padded, norm_params, dense, router_wide
+    )
+    tokens = images * PAD
+    x, g, xt, gt = dispatch(
+        slot_row, second.reshape(tokens, model_width), upstream.reshape(tokens, model_width),
+        route_probs.reshape(tokens, 128), experts, slots,
+    )
+    sums = None
+    expert_sums = []
+    for i in range(parts):
+        made, back, grads = run_experts(
+            expert_places[i], x, g, xt, gt, sums, expert_pieces[i], i == parts - 1
+        )
+        sums = (made, back)
+        expert_sums.append(collect(grads, expert_stages[i]))
+    block_output, hidden_grad, router_part, norm_two = combine(
+        length, experts, slot_column, made, back, hidden, upstream, second, route_probs,
+        norm_params, router_wide,
+    )
+    input_grad, norm_one, dense_grads = attend_back(
+        length, dense_places, padded, norm_params, dense, normed, projected, probs, context,
+        hidden_grad, dense_pieces.shape,
+    )
+    dense_sum = collect(dense_grads, dense_stages).astype(jnp.float32)
+    small = sum_all(
+        jnp.concatenate([(norm_one + norm_two)[:4], router_part[:experts]]), dense_stages
+    )
+    norm_grad, router_grad = small[:4], small[4:].T
+    qkv_grad, attn_grad = dense_sum[:3].transpose(1, 0, 2), dense_sum[3].T
+    expert_sum = jnp.concatenate(expert_sums, axis=2).astype(jnp.float32)
+    in_grad, out_grad = expert_sum[0][None], expert_sum[1].T[None]
+    norm_new = adam_update(norm_params, norm_grad, norm_moment, norm_square, 0.25, 0.0)
+    qkv_new = adam_update(
+        qkv_weight, qkv_grad, qkv_moment, qkv_square, 1.3 * model_width ** (-0.5), DECAY_RATE
+    )
+    attn_new = adam_update(
+        attn_weight, attn_grad, attn_moment, attn_square, 3.0 * model_width ** (-0.5), DECAY_RATE
+    )
+    router_new = adam_update(
+        router_weight,
+        router_grad,
+        router_moment,
+        router_square,
+        0.75 * model_width ** (-0.5),
+        DECAY_RATE,
+    )
+    in_new = adam_update(
+        expert_in, in_grad, in_moment, in_square, 1.0 * model_width ** (-0.5), DECAY_RATE
+    )
+    out_new = adam_update(
+        expert_out, out_grad, out_moment, out_square, 0.8 * experts * FF ** (-0.5), DECAY_RATE
+    )
+    return (
+        block_output,
+        input_grad,
+        norm_new[0],
+        norm_new[1],
+        norm_new[2],
+        qkv_new[0],
+        qkv_new[1],
+        qkv_new[2],
+        attn_new[0],
+        attn_new[1],
+        attn_new[2],
+        router_new[0],
+        router_new[1],
+        router_new[2],
+        in_new[0],
+        in_new[1],
+        in_new[2],
+        out_new[0],
+        out_new[1],
+        out_new[2],
+    )
+
+
 def solution(mesh):
+    fits = mesh.shape["shard"] <= 4
     return jax.shard_map(
-        on_device,
+        local_plan if fits else slot_plan,
         mesh=mesh,
         in_specs=(
             P(("shard", "head", "tensor"), None, None),

time: 1220 us -> 532 us (0.44)
  waiting for transfers between devices: 616 us -> 210 us
  matrix products: 153 us -> 0 us
  blocking collectives: 148 us -> 0 us
  Pallas kernels: 0 us -> 146 us
  local copies, waits for them, and re-layouts: 167 us -> 78.9 us
  other arithmetic: 83.5 us -> 42.3 us
  starting transfers between devices: 23.2 us -> 43.1 us
  between operations: 16 us -> 2.06 us
    all_to_all x4 -> x0, waiting for transfers between devices: 379 us -> none  [the longest x2 199 us: return_rows(): lax.all_to_all(flat_rows.astype(jnp.bfloat16), ('shard', 'tensor'), split...]
    ppermute x0 -> x35, waiting for transfers between devices: none -> 210 us  [relay(): return lax.ppermute(block, axis, [(i, i ^ mask) for i in range(size)])]
    reduce_scatter x4 -> x0, waiting for transfers between devices: 153 us -> none  [the longest x1 64.1 us: on_device(): lax.psum_scatter(qkv_grad, ('shard', 'tensor'), scatter_dimension=0, tile...]
    dot_general x22 -> x0, matrix products: 153 us -> none  [the longest x1 21.8 us: on_device(): jnp.einsum('stecd,efd->stecf', grad_arrived, hidden_out, preferred_elemen...]
    pallas_call x0 -> x8, Pallas kernels: none -> 146 us  [the longest x2 59.9 us: run_experts(): pl.pallas_call(partial(expert_kernel, first, last), grid=(experts,), in_s...]
    all_gather x2 -> x0, blocking collectives: 63.3 us -> none  [the longest x1 32.4 us: on_device(): lax.all_gather(attn_weight.astype(jnp.bfloat16), ('shard', 'tensor'), axi...]
    all_gather x4 -> x0, waiting for transfers between devices: 60 us -> none  [the longest x1 23.6 us: on_device(): lax.all_gather(hidden_grad.astype(jnp.bfloat16), 'head', axis=0, tiled=True)]
    reduce_sum x14 -> x0, other arithmetic: 47.6 us -> none  [the longest x1 16.8 us: on_device(): gate_grad = jnp.sum(upstream[:, None, :] * per_pair, axis=-1)]
  transfers between devices with their start and end apart: 14 -> 35, of which waited for: 11 -> 20; matrix products, arithmetic and copies ran while one was open for 16% -> 20% of each run, Pallas kernels for 0% -> 28%
where the time goes in v1:
time: 532 us; the launch traced here: 522 us
  waiting for transfers between devices  210 us (39%)
  Pallas kernels  146 us (27%)
  local copies, waits for them, and re-layouts  78.9 us (15%)
  starting transfers between devices  43.1 us (8%)
  other arithmetic  42.3 us (8%)
    ppermute x35, waiting for transfers between devices, relay(): return lax.ppermute(block, axis, [(i, i ^ mask) for i in range(size)])  210 us
    pallas_call x2, Pallas kernels, run_experts(): pl.pallas_call(partial(expert_kernel, first, last), grid=(experts,), in_s...  59.9 us
    ppermute x35, starting transfers between devices, relay(): return lax.ppermute(block, axis, [(i, i ^ mask) for i in range(size)])  43.1 us
    unnamed x125, local copies, waits for them, and re-layouts  34.8 us
    pallas_call x1, Pallas kernels, attend_back(): pl.pallas_call(attend_back_kernel, grid=(images,), in_specs=[pl.BlockSpec...  31.7 us
    concatenate x6, local copies, waits for them, and re-layouts, spread(): pieces = jnp.concatenate([pieces, relay(pieces, axis, mask)], axis=0)  18.7 us
    pallas_call x1, Pallas kernels, attend(): pl.pallas_call(partial(attend_kernel, length, experts), grid=(images,), i...  17.2 us
    convert_element_type x12, other arithmetic, collect(): pieces = total.astype(pieces.dtype)  16.5 us
  transfers between devices with their start and end apart: 35, of which 20 were waited for; matrix products, arithmetic and copies ran while one was open for 20% of the time, Pallas kernels for 28%

profile of v1, /device:TPU:0, one launch (start us, length us, event | category | flops | bytes accessed | tf_op | source)
XLA Modules:
  0.0 522.0 jit_solution(17050713989708527792)
XLA Ops:
  4.2 3.0 collective-permute-start.5
  7.2 6.3 %collective-permute-done.5 = bf16[1,2,128,512]{3,2,1,0:T(8,128)(2,1)S(1)} collective-permute-done((bf16[1,2,128,512]{3,2,1,0:T(8,128)(2,1)S(1)}, bf16[1,2,128,512]{3,2,1,0:T(8,128)(2,1)S(1)}, u32[]{:S(2)}, u32[]{:S(2)}) %collective-permute-start.5) | collective-permute-done | bytes 262176 | tf_op jit(solution)/shard_map/ppermute | solution.py:894
  13.5 2.8 collective-permute-start.6
  16.4 1.6 collective-permute-start.10
  17.9 20.9 %collective-permute-done.6 = bf16[2,2,128,512]{3,2,1,0:T(8,128)(2,1)S(1)} collective-permute-done((bf16[2,2,128,512]{3,2,1,0:T(8,128)(2,1)S(1)}, bf16[2,2,128,512]{3,2,1,0:T(8,128)(2,1)S(1)}, u32[]{:S(2)}, u32[]{:S(2)}) %collective-permute-start.6) | collective-permute-done | bytes 524320 | tf_op jit(solution)/shard_map/ppermute | solution.py:894
  46.1 3.4 collective-permute-start.11
  54.1 10.3 %collective-permute-done.7 = bf16[4,2,128,512]{3,2,1,0:T(8,128)(2,1)} collective-permute-done((bf16[4,2,128,512]{3,2,1,0:T(8,128)(2,1)}, bf16[4,2,128,512]{3,2,1,0:T(8,128)(2,1)}, u32[]{:S(2)}, u32[]{:S(2)}) %collective-permute-start.7) | collective-permute-done | bytes 1048608 | tf_op jit(solution)/shard_map/ppermute | solution.py:894
  64.5 2.9 pad_maximum_fusion
  68.6 3.7 collective-permute-done.11
  72.3 2.1 pad_maximum_fusion.3
  74.5 1.5 collective-permute-start.12
  76.0 10.8 %find_slots.1 = (s32[8,1248]{1,0:T(8,128)S(1)}, s32[1248,128]{1,0:T(8,128)S(1)}) custom-call(s32[8,1248]{1,0:T(8,128)S(1)} %copy.79.row_ref, s32[1248,8]{1,0:T(8,128)S(1)} %get-tuple-element.182.column_ref), custom_call_target="tpu_custom_call" | custom-call | flops 10000000000 | bytes 1000000 | tf_op jit(solution)/shard_map/find_slots/pallas_call | solution.py:413
  90.0 6.9 %collective-permute-done.1 = bf16[2,4,64,128]{3,2,1,0:T(8,128)(2,1)S(1)} collective-permute-done((bf16[2,4,64,128]{3,2,1,0:T(8,128)(2,1)S(1)}, bf16[2,4,64,128]{3,2,1,0:T(8,128)(2,1)S(1)}, u32[]{:S(2)}, u32[]{:S(2)}) %collective-permute-start.1) | collective-permute-done | bytes 131104 | tf_op jit(solution)/shard_map/ppermute | solution.py:894
  98.4 1.7 constant_dynamic-update-slice_fusion.14
  100.1 35.8 %collective-permute-done.12 = bf16[4,2,128,512]{3,2,1,0:T(8,128)(2,1)} collective-permute-done((bf16[4,2,128,512]{3,2,1,0:T(8,128)(2,1)}, bf16[4,2,128,512]{3,2,1,0:T(8,128)(2,1)}, u32[]{:S(2)}, u32[]{:S(2)}) %collective-permute-start.12) | collective-permute-done | bytes 1048608 | tf_op jit(solution)/shard_map/ppermute | solution.py:894
  135.9 3.0 pad_maximum_fusion.1
  140.8 2.6 constant_dynamic-update-slice_fusion.12
  143.5 3.5 constant_dynamic-update-slice_fusion.11
  147.0 2.3 pad_maximum_fusion.4
  150.5 1.5 collective-permute-start.3
  152.0 1.5 constant_dynamic-update-slice_fusion.3
  155.0 8.2 %collective-permute-done.3 = bf16[8,4,64,128]{3,2,1,0:T(8,128)(2,1)S(1)} collective-permute-done((bf16[8,4,64,128]{3,2,1,0:T(8,128)(2,1)}, bf16[8,4,64,128]{3,2,1,0:T(8,128)(2,1)S(1)}, u32[]{:S(2)}, u32[]{:S(2)}) %collective-permute-start.3) | collective-permute-done | bytes 524320 | tf_op jit(solution)/shard_map/ppermute | solution.py:894
  167.8 2.5 pad.24.upstream_ref
  170.9 1.8 constant_dynamic-update-slice_fusion.25
  172.7 2.1 constant_dynamic-update-slice_fusion.24
  174.8 2.8 constant_dynamic-update-slice_fusion.23
  177.6 6.4 %collective-permute-done.13 = bf16[8,2,128,512]{3,2,1,0:T(8,128)(2,1)} collective-permute-done((bf16[8,2,128,512]{3,2,1,0:T(8,128)(2,1)}, bf16[8,2,128,512]{3,2,1,0:T(8,128)(2,1)}, u32[]{:S(2)}, u32[]{:S(2)}) %collective-permute-start.13) | collective-permute-done | bytes 2097184 | tf_op jit(solution)/shard_map/ppermute | solution.py:894
  184.0 4.2 constant_dynamic-update-slice_fusion.22
  192.9 17.2 %attend.1 = (bf16[6,208,512]{2,1,0:T(8,128)(2,1)S(1)}, bf16[6,3,208,512]{3,2,1,0:T(8,128)(2,1)}, bf16[6,8,208,208]{3,2,1,0:T(8,128)(2,1)}, bf16[6,208,512]{2,1,0...) custom-call(bf16[6,208,512]{2,1,0:T(8,128)(2,1)S(1)} %pad.22.input_ref, ...), custom_call_target="tpu_custom_call" | custom-call | flops 15000000512 | bytes 30000000 | tf_op jit(solution)/shard_map/attend/pallas_call | solution.py:519
  212.3 9.3 %dispatch.1 = (bf16[4,672,512]{2,1,0:T(8,128)(2,1)S(1)}, bf16[4,672,512]{2,1,0:T(8,128)(2,1)}, bf16[4,512,672]{2,1,0:T(8,128)(2,1)}, bf16[4,512,672]{2,1,0:T(8,128)(2,1)}) custom-call(s32[8,1248]{1,0:T(8,128)S(1)} %copy-done.12, bf16[1248,512]{1,0:T(8,128)(2,1)S(1)} %bitcast.78, bf16[1248,512]{1,0:T(8,128)(2,1)S(1)} %bitcast.77, f32[1248,128]{1,0:T(8,128)S(1)} %bitcast.80), custom_call_target="tpu_custom_call" | custom-call | flops 6870269952 | bytes 10000000 | tf_op jit(solution)/shard_map/dispatch/pallas_call | solution.py:559
  221.7 3.9 constant_dynamic-update-slice_fusion.16.refs_0_
  225.6 3.3 copy-done.44
  228.9 29.3 %experts.2 = (f32[4,672,512]{2,1,0:T(8,128)}, f32[4,672,512]{2,1,0:T(8,128)}, bf16[32,2,128,512]{3,2,1,0:T(8,128)(2,1)}) custom-call(s32[4,8]{1,0:T(4,128)} %get-tuple-element.205.place_ref, bf16[4,672,512]{2,1,0:T(8,128)(2,1)} %copy-done.8, bf16[4,672,512]{2,1,0:T(8,128)(2,1)} %get-tuple-element.51.g_ref, bf16[4,512,672]{2,1,0:T(8,128)(2,1)} %get-tuple-element.52.xt_ref, ...), custom_call_target="tpu_custom_call" | custom-call | flops 16911433728 | bytes 30000000 | tf_op jit(solution)/shard_map/experts/pallas_call | solution.py:676
  258.2 4.7 slice.144
  263.4 4.6 constant_dynamic-update-slice_fusion.27.refs_2_
  268.0 30.6 %experts.3 = (bf16[4,672,512]{2,1,0:T(8,128)(2,1)}, bf16[4,672,512]{2,1,0:T(8,128)(2,1)}, bf16[32,2,128,512]{3,2,1,0:T(8,128)(2,1)}) custom-call(s32[4,8]{1,0:T(4,128)} %get-tuple-element.206.place_ref, bf16[4,672,512]{2,1,0:T(8,128)(2,1)} %copy-done.8, bf16[4,672,512]{2,1,0:T(8,128)(2,1)} %get-tuple-element.51.g_ref, ...), custom_call_target="tpu_custom_call" | custom-call | flops 16911433728 | bytes 30000000 | tf_op jit(solution)/shard_map/experts/pallas_call | solution.py:676
  298.6 4.7 slice.154
  303.4 15.6 %combine.1 = (bf16[6,197,512]{2,1,0:T(8,128)(2,1)}, f32[6,208,512]{2,1,0:T(8,128)}, f32[8,512]{1,0:T(8,128)S(1)}, f32[8,512]{1,0:T(8,128)S(1)}) custom-call(s32[6,208,128]{2,1,0:T(8,128)S(1)} %bitcast.79, bf16[4,672,512]{2,1,0:T(8,128)(2,1)} %get-tuple-element.56.made_ref, bf16[4,672,512]{2,1,0:T(8,128)(2,1)} %get-tuple-element.57.back_ref, ...), custom_call_target="tpu_custom_call" | custom-call | flops 6870269952 | bytes 20000000 | tf_op jit(solution)/shard_map/combine/pallas_call | solution.py:756
  318.9 31.7 %attend_back.1 = (f32[6,197,512]{2,1,0:T(8,128)}, f32[8,512]{1,0:T(8,128)}, bf16[32,4,64,128]{3,2,1,0:T(8,128)(2,1)}) custom-call(s32[32]{0:T(128)} %copy-done.5, bf16[6,208,512]{2,1,0:T(8,128)(2,1)} %copy-done.1, f32[4,512]{1,0:T(4,128)} %norm_ref.5, bf16[4,512,512]{2,1,0:T(8,128)(2,1)} %copy-done, bf16[6,208,512]{2,1,0:T(8,128)(2,1)} %copy-done.9, ...), custom_call_target="tpu_custom_call" | custom-call | flops 30000001024 | bytes 36000000 | tf_op jit(solution)/shard_map/attend_back/pallas_call | solution.py:864
  350.7 1.4 slice.130
  352.7 5.4 %add_convert_fusion.1 = bf16[16,2,128,512]{3,2,1,0:T(8,128)(2,1)S(1)} fusion(bf16[16,2,128,512]{3,2,1,0:T(8,128)(2,1)} %collective-permute-done.25, bf16[32,2,128,512]{3,2,1,0:T(8,128)(2,1)} %get-tuple-element.70), kind=kLoop, calls=%fused_computation.1 | loop fusion | flops 8388608 | bytes 12582912 | tf_op jit(solution)/shard_map/convert_element_type | solution.py:909
  358.1 1.6 slice.182
  360.4 3.7 add_convert_fusion
  365.6 1.5 collective-permute-start.31
  369.8 3.4 collective-permute-start.15
  373.3 1.7 collective-permute-done.15
  375.0 3.5 collective-permute-start.16
  378.5 1.7 collective-permute-done.16
  380.2 1.5 collective-permute-start.17
  381.7 31.6 %collective-permute-done.17 = f32[8,512]{1,0:T(8,128)S(1)} collective-permute-done((f32[8,512]{1,0:T(8,128)S(1)}, f32[8,512]{1,0:T(8,128)S(1)}, u32[]{:S(2)}, u32[]{:S(2)}) %collective-permute-start.17) | collective-permute-done | bytes 16416 | tf_op jit(solution)/shard_map/ppermute | solution.py:894
  414.5 4.3 collective-permute-done.18
  418.8 2.0 copy.82
  420.9 2.0 copy.83
  425.1 2.6 add_convert_fusion.3
  428.8 2.3 add_convert_fusion.2
  434.2 5.2 collective-permute-done.23
  439.5 4.5 collective-permute-start.24
  444.0 11.5 %collective-permute-done.27 = bf16[4,2,128,512]{3,2,1,0:T(8,128)(2,1)S(1)} collective-permute-done((bf16[4,2,128,512]{3,2,1,0:T(8,128)(2,1)S(1)}, bf16[4,2,128,512]{3,2,1,0:T(8,128)(2,1)S(1)}, u32[]{:S(2)}, u32[]{:S(2)}) %collective-permute-start.27) | collective-permute-done | bytes 1048608 | tf_op jit(solution)/shard_map/ppermute | solution.py:894
  456.9 2.4 collective-permute-start.33
  460.1 34.0 %collective-permute-done.28 = bf16[2,2,128,512]{3,2,1,0:T(8,128)(2,1)S(1)} collective-permute-done((bf16[2,2,128,512]{3,2,1,0:T(8,128)(2,1)S(1)}, bf16[2,2,128,512]{3,2,1,0:T(8,128)(2,1)S(1)}, u32[]{:S(2)}, u32[]{:S(2)}) %collective-permute-start.28) | collective-permute-done | bytes 524320 | tf_op jit(solution)/shard_map/ppermute | solution.py:894
  494.3 9.8 %collective-permute-done.33 = bf16[2,2,128,512]{3,2,1,0:T(8,128)(2,1)S(1)} collective-permute-done((bf16[2,2,128,512]{3,2,1,0:T(8,128)(2,1)S(1)}, bf16[2,2,128,512]{3,2,1,0:T(8,128)(2,1)S(1)}, u32[]{:S(2)}, u32[]{:S(2)}) %collective-permute-start.33) | collective-permute-done | bytes 524320 | tf_op jit(solution)/shard_map/ppermute | solution.py:894
  505.1 4.7 collective-permute-done.29
  509.8 5.5 %collective-permute-done.34 = bf16[1,2,128,512]{3,2,1,0:T(8,128)(2,1)S(1)} collective-permute-done((bf16[1,2,128,512]{3,2,1,0:T(8,128)(2,1)S(1)}, bf16[1,2,128,512]{3,2,1,0:T(8,128)(2,1)S(1)}, u32[]{:S(2)}, u32[]{:S(2)}) %collective-permute-start.34) | collective-permute-done | bytes 262176 | tf_op jit(solution)/shard_map/ppermute | solution.py:894
  518.9 2.6 multiply_subtract_fusion.1
  (236 shorter events, 58.3 us)
Async XLA Ops:
  0.7 40.7 %copy-start.29 = (f32[64,3,128]{2,0,1:T(8,128)S(1)}, f32[64,3,128]{2,0,1:T(8,128)}, u32[]{:S(2)}) copy-start(f32[64,3,128]{2,0,1:T(8,128)} %param.29) | copy-start | bytes 294916
  0.7 40.7 %copy-start.31 = (f32[128,64]{0,1:T(8,128)S(1)}, f32[128,64]{0,1:T(8,128)}, u32[]{:S(2)}) copy-start(f32[128,64]{0,1:T(8,128)} %param.32) | copy-start | bytes 98308
  0.7 42.1 %copy-start.38 = (s32[1,2364]{1,0:T(1,128)S(1)}, s32[1,2364]{1,0:T(1,128)}, u32[]{:S(2)}) copy-start(s32[1,2364]{1,0:T(1,128)} %param.25) | copy-start | bytes 28372
  2.0 39.4 %copy-start.16 = (f32[1,1024,128]{1,2,0:T(8,128)}, f32[1,1024,128]{1,2,0:T(8,128)S(1)}, u32[]{:S(2)}) copy-start(f32[1,1024,128]{1,2,0:T(8,128)S(1)} %copy.81) | copy-start | bytes 1572868
  4.2 9.3 %collective-permute-start.5 = (bf16[1,2,128,512]{3,2,1,0:T(8,128)(2,1)S(1)}, bf16[1,2,128,512]{3,2,1,0:T(8,128)(2,1)S(1)}, u32[]{:S(2)}, u32[]{:S(2)}) collective-permute-start(bf16[1,2,128,512]{3,2,1,0:T(8,128)(2,1)S(1)} %get-tuple-element.187), channel_id=1, source_target_pairs={{0,8},{8,0},{16,24},{24,16},{1,9},{9,1},{17,25},{25,17},{2,10},{10... | collective-permute-start | bytes 786440 | tf_op jit(solution)/shard_map/ppermute | solution.py:894
  13.5 27.9 %copy-start.22 = (bf16[1,2,128,512]{3,2,1,0:T(8,128)(2,1)}, bf16[1,2,128,512]{3,2,1,0:T(8,128)(2,1)S(1)}, u32[]{:S(2)}) copy-start(bf16[1,2,128,512]{3,2,1,0:T(8,128)(2,1)S(1)} %collective-permute-done.5) | copy-start | bytes 786436
  13.5 25.3 %collective-permute-start.6 = (bf16[2,2,128,512]{3,2,1,0:T(8,128)(2,1)S(1)}, bf16[2,2,128,512]{3,2,1,0:T(8,128)(2,1)S(1)}, u32[]{:S(2)}, u32[]{:S(2)}) collective-permute-start(bf16[2,2,128,512]{3,2,1,0:T(8,128)(2,1)S(1)} %pad_maximum_fusion.5), channel_id=1, source_target_pairs={{0,16},{8,24},{16,0},{24,8},{1,17},{9,25},{17,1},{25,9},{2,18},{10... | collective-permute-start | bytes 1572872 | tf_op jit(solution)/shard_map/ppermute | solution.py:894
  16.4 28.9 %collective-permute-start.10 = (bf16[1,2,128,512]{3,2,1,0:T(8,128)(2,1)S(1)}, bf16[1,2,128,512]{3,2,1,0:T(8,128)(2,1)S(1)}, u32[]{:S(2)}, u32[]{:S(2)}) collective-permute-start(bf16[1,2,128,512]{3,2,1,0:T(8,128)(2,1)S(1)} %get-tuple-element.171), channel_id=1, source_target_pairs={{0,8},{8,0},{16,24},{24,16},{1,9},{9,1},{17,25},{25,17},{2,10},{10... | collective-permute-start | bytes 786440 | tf_op jit(solution)/shard_map/ppermute | solution.py:894
  40.0 24.5 %collective-permute-start.7 = (bf16[4,2,128,512]{3,2,1,0:T(8,128)(2,1)}, bf16[4,2,128,512]{3,2,1,0:T(8,128)(2,1)}, u32[]{:S(2)}, u32[]{:S(2)}) collective-permute-start(bf16[4,2,128,512]{3,2,1,0:T(8,128)(2,1)} %pad_maximum_fusion.2), channel_id=1, source_target_pairs={{0,4},{2,6},{4,0},{6,2},{1,5},{3,7},{5,1},{7,3},{8,12},{10,14},{12... | collective-permute-start | bytes 3145736 | tf_op jit(solution)/shard_map/ppermute | solution.py:894
  42.1 46.1 %collective-permute-start = (bf16[1,4,64,128]{3,2,1,0:T(8,128)(2,1)}, bf16[1,4,64,128]{3,2,1,0:T(8,128)(2,1)}, u32[]{:S(2)}, u32[]{:S(2)}) collective-permute-start(bf16[1,4,64,128]{3,2,1,0:T(8,128)(2,1)} %get-tuple-element.204), channel_id=1, source_target_pairs={{0,8},{8,0},{16,24},{24,16},{1,9},{9,1},{17,25},{25,17},{2,10},{10... | collective-permute-start | bytes 196616 | tf_op jit(solution)/shard_map/ppermute | solution.py:894
  45.3 6.7 %copy-start.20 = (bf16[1,2,128,512]{3,2,1,0:T(8,128)(2,1)}, bf16[1,2,128,512]{3,2,1,0:T(8,128)(2,1)S(1)}, u32[]{:S(2)}) copy-start(bf16[1,2,128,512]{3,2,1,0:T(8,128)(2,1)S(1)} %collective-permute-done.10) | copy-start | bytes 786436
  46.1 26.2 %collective-permute-start.11 = (bf16[2,2,128,512]{3,2,1,0:T(8,128)(2,1)}, bf16[2,2,128,512]{3,2,1,0:T(8,128)(2,1)}, u32[]{:S(2)}, u32[]{:S(2)}) collective-permute-start(bf16[2,2,128,512]{3,2,1,0:T(8,128)(2,1)} %pad_maximum_fusion.6), channel_id=1, source_target_pairs={{0,16},{8,24},{16,0},{24,8},{1,17},{9,25},{17,1},{25,9},{2,18},{10... | collective-permute-start | bytes 1572872 | tf_op jit(solution)/shard_map/ppermute | solution.py:894
  54.1 18.2 %copy-start.21 = (bf16[1,2,128,512]{3,2,1,0:T(8,128)(2,1)S(1)}, bf16[1,2,128,512]{3,2,1,0:T(8,128)(2,1)}, u32[]{:S(2)}) copy-start(bf16[1,2,128,512]{3,2,1,0:T(8,128)(2,1)} %copy-done.20) | copy-start | bytes 786436
  67.4 76.0 %collective-permute-start.8 = (bf16[8,2,128,512]{3,2,1,0:T(8,128)(2,1)}, bf16[8,2,128,512]{3,2,1,0:T(8,128)(2,1)}, u32[]{:S(2)}, u32[]{:S(2)}) collective-permute-start(bf16[8,2,128,512]{3,2,1,0:T(8,128)(2,1)} %pad_maximum_fusion), channel_id=1, source_target_pairs={{0,1},{1,0},{2,3},{3,2},{4,5},{5,4},{6,7},{7,6},{8,9},{9,8},{10,11... | collective-permute-start | bytes 6291464 | tf_op jit(solution)/shard_map/ppermute | solution.py:894
  74.5 61.4 %collective-permute-start.12 = (bf16[4,2,128,512]{3,2,1,0:T(8,128)(2,1)}, bf16[4,2,128,512]{3,2,1,0:T(8,128)(2,1)}, u32[]{:S(2)}, u32[]{:S(2)}) collective-permute-start(bf16[4,2,128,512]{3,2,1,0:T(8,128)(2,1)} %pad_maximum_fusion.3), channel_id=1, source_target_pairs={{0,1},{1,0},{2,3},{3,2},{4,5},{5,4},{6,7},{7,6},{8,9},{9,8},{10,11... | collective-permute-start | bytes 3145736 | tf_op jit(solution)/shard_map/ppermute | solution.py:894
  76.0 12.2 %copy-start.28 = (bf16[1,1,64,128]{3,2,1,0:T(8,128)(2,1)S(1)}, bf16[1,1,64,128]{3,2,1,0:T(8,128)(2,1)}, u32[]{:S(2)}) copy-start(bf16[1,1,64,128]{3,2,1,0:T(8,128)(2,1)} %copy-done.27) | copy-start | bytes 49156
  88.2 51.7 %copy-start.19 = (bf16[2,2,128,512]{3,2,1,0:T(8,128)(2,1)S(1)}, bf16[2,2,128,512]{3,2,1,0:T(8,128)(2,1)}, u32[]{:S(2)}) copy-start(bf16[2,2,128,512]{3,2,1,0:T(8,128)(2,1)} %copy-done.18) | copy-start | bytes 1572868
  89.1 7.8 %collective-permute-start.1 = (bf16[2,4,64,128]{3,2,1,0:T(8,128)(2,1)S(1)}, bf16[2,4,64,128]{3,2,1,0:T(8,128)(2,1)S(1)}, u32[]{:S(2)}, u32[]{:S(2)}) collective-permute-start(bf16[2,4,64,128]{3,2,1,0:T(8,128)(2,1)S(1)} %pad_maximum_fusion.9), channel_id=1, source_target_pairs={{0,16},{8,24},{16,0},{24,8},{1,17},{9,25},{17,1},{25,9},{2,18},{10... | collective-permute-start | bytes 393224 | tf_op jit(solution)/shard_map/ppermute | solution.py:894
  89.2 75.1 %copy-start.46 = (s32[4]{0:T(128)}, s32[4]{0:T(128)S(1)}, u32[]{:S(2)}) copy-start(s32[4]{0:T(128)S(1)} %get-tuple-element.209) | copy-start | bytes 52
  89.2 75.1 %copy-start.48 = (s32[4]{0:T(128)}, s32[4]{0:T(128)S(1)}, u32[]{:S(2)}) copy-start(s32[4]{0:T(128)S(1)} %get-tuple-element.210) | copy-start | bytes 52
  97.8 49.2 %collective-permute-start.2 = (bf16[4,4,64,128]{3,2,1,0:T(8,128)(2,1)S(1)}, bf16[4,4,64,128]{3,2,1,0:T(8,128)(2,1)S(1)}, u32[]{:S(2)}, u32[]{:S(2)}) collective-permute-start(bf16[4,4,64,128]{3,2,1,0:T(8,128)(2,1)S(1)} %pad_maximum_fusion.8), channel_id=1, source_target_pairs={{0,4},{2,6},{4,0},{6,2},{1,5},{3,7},{5,1},{7,3},{8,12},{10,14},{12... | collective-permute-start | bytes 786440 | tf_op jit(solution)/shard_map/ppermute | solution.py:894
  138.9 45.1 %collective-permute-start.13 = (bf16[8,2,128,512]{3,2,1,0:T(8,128)(2,1)}, bf16[8,2,128,512]{3,2,1,0:T(8,128)(2,1)}, u32[]{:S(2)}, u32[]{:S(2)}) collective-permute-start(bf16[8,2,128,512]{3,2,1,0:T(8,128)(2,1)} %pad_maximum_fusion.1), channel_id=1, source_target_pairs={{0,4},{2,6},{4,0},{6,2},{1,5},{3,7},{5,1},{7,3},{8,12},{10,14},{12... | collective-permute-start | bytes 6291464 | tf_op jit(solution)/shard_map/ppermute | solution.py:894
  143.5 21.1 %copy-start.37 = (f32[512,4]{0,1:T(4,128)S(1)}, f32[512,4]{0,1:T(4,128)}, u32[]{:S(2)}) copy-start(f32[512,4]{0,1:T(4,128)} %param.35) | copy-start | bytes 24580
  147.0 74.7 %collective-permute-start.9 = (bf16[16,2,128,512]{3,2,1,0:T(8,128)(2,1)}, bf16[16,2,128,512]{3,2,1,0:T(8,128)(2,1)}, u32[]{:S(2)}, u32[]{:S(2)}) collective-permute-start(bf16[16,2,128,512]{3,2,1,0:T(8,128)(2,1)} %get-tuple-element.176), channel_id=1, source_target_pairs={{0,2},{2,0},{4,6},{6,4},{1,3},{3,1},{5,7},{7,5},{8,10},{10,8},{12,... | collective-permute-start | bytes 12582920 | tf_op jit(solution)/shard_map/ppermute | solution.py:894
  150.5 12.7 %collective-permute-start.3 = (bf16[8,4,64,128]{3,2,1,0:T(8,128)(2,1)}, bf16[8,4,64,128]{3,2,1,0:T(8,128)(2,1)S(1)}, u32[]{:S(2)}, u32[]{:S(2)}) collective-permute-start(bf16[8,4,64,128]{3,2,1,0:T(8,128)(2,1)} %pad_maximum_fusion.4), channel_id=1, source_target_pairs={{0,1},{1,0},{2,3},{3,2},{4,5},{5,4},{6,7},{7,6},{8,9},{9,8},{10,11... | collective-permute-start | bytes 1572872 | tf_op jit(solution)/shard_map/ppermute | solution.py:894
  164.3 24.5 %collective-permute-start.4 = (bf16[16,4,64,128]{3,2,1,0:T(8,128)(2,1)}, bf16[16,4,64,128]{3,2,1,0:T(8,128)(2,1)}, u32[]{:S(2)}, u32[]{:S(2)}) collective-permute-start(bf16[16,4,64,128]{3,2,1,0:T(8,128)(2,1)} %get-tuple-element.190), channel_id=1, source_target_pairs={{0,2},{2,0},{4,6},{6,4},{1,3},{3,1},{5,7},{7,5},{8,10},{10,8},{12,... | collective-permute-start | bytes 3145736 | tf_op jit(solution)/shard_map/ppermute | solution.py:894
  164.5 25.7 %copy-start.5 = (s32[32]{0:T(128)}, s32[32]{0:T(128)S(1)}, u32[]{:S(2)}) copy-start(s32[32]{0:T(128)S(1)} %reshape.170.place_ref) | copy-start | bytes 388
  166.7 24.8 %copy-start.1 = (bf16[6,208,512]{2,1,0:T(8,128)(2,1)}, bf16[6,208,512]{2,1,0:T(8,128)(2,1)S(1)}, u32[]{:S(2)}) copy-start(bf16[6,208,512]{2,1,0:T(8,128)(2,1)S(1)} %pad.22.input_ref) | copy-start | bytes 3833860
  188.2 75.2 %collective-permute-start.14 = (bf16[16,2,128,512]{3,2,1,0:T(8,128)(2,1)}, bf16[16,2,128,512]{3,2,1,0:T(8,128)(2,1)}, u32[]{:S(2)}, u32[]{:S(2)}) collective-permute-start(bf16[16,2,128,512]{3,2,1,0:T(8,128)(2,1)} %get-tuple-element.174), channel_id=1, source_target_pairs={{0,2},{2,0},{4,6},{6,4},{1,3},{3,1},{5,7},{7,5},{8,10},{10,8},{12,... | collective-permute-start | bytes 12582920 | tf_op jit(solution)/shard_map/ppermute | solution.py:894
  190.2 31.4 %slice-start.2 = ((s8[8388608]{0:T(1024)(128)(4,1)}), s8[4194304]{0:T(1024)(128)(4,1)S(1)}, s32[]{:S(2)}) async-start(s8[8388608]{0:T(1024)(128)(4,1)} %bitcast.84), calls=%async_computation.2 | async-start | bytes 8388608
  192.9 19.4 %copy-start.2 = (bf16[6,208,512]{2,1,0:T(8,128)(2,1)S(1)}, bf16[6,208,512]{2,1,0:T(8,128)(2,1)}, u32[]{:S(2)}) copy-start(bf16[6,208,512]{2,1,0:T(8,128)(2,1)} %pad.24.upstream_ref) | copy-start | bytes 3833860
  192.9 19.4 %copy-start.12 = (s32[8,1248]{1,0:T(8,128)S(1)}, s32[8,1248]{1,0:T(8,128)}, u32[]{:S(2)}) copy-start(s32[8,1248]{1,0:T(8,128)} %copy-done.11) | copy-start | bytes 119812
  192.9 28.7 %slice-start.3 = ((s8[8388608]{0:T(1024)(128)(4,1)}), s8[4194304]{0:T(1024)(128)(4,1)S(1)}, s32[]{:S(2)}) async-start(s8[8388608]{0:T(1024)(128)(4,1)} %bitcast.84), calls=%async_computation.3 | async-start | bytes 8388608
  262.9 89.9 %collective-permute-start.25 = (bf16[16,2,128,512]{3,2,1,0:T(8,128)(2,1)}, bf16[16,2,128,512]{3,2,1,0:T(8,128)(2,1)}, u32[]{:S(2)}, u32[]{:S(2)}) collective-permute-start(bf16[16,2,128,512]{3,2,1,0:T(8,128)(2,1)} %slice.144), channel_id=1, source_target_pairs={{0,2},{2,0},{4,6},{6,4},{1,3},{3,1},{5,7},{7,5},{8,10},{10,8},{12,... | collective-permute-start | bytes 12582920 | tf_op jit(solution)/shard_map/ppermute | solution.py:894
  303.4 57.1 %collective-permute-start.30 = (bf16[16,2,128,512]{3,2,1,0:T(8,128)(2,1)}, bf16[16,2,128,512]{3,2,1,0:T(8,128)(2,1)}, u32[]{:S(2)}, u32[]{:S(2)}) collective-permute-start(bf16[16,2,128,512]{3,2,1,0:T(8,128)(2,1)} %slice.154), channel_id=1, source_target_pairs={{0,2},{2,0},{4,6},{6,4},{1,3},{3,1},{5,7},{7,5},{8,10},{10,8},{12,... | collective-permute-start | bytes 12582920 | tf_op jit(solution)/shard_map/ppermute | solution.py:894
  350.7 9.7 %slice-start = ((s8[8388608]{0:T(1024)(128)(4,1)}), s8[4194304]{0:T(1024)(128)(4,1)S(1)}, s32[]{:S(2)}) async-start(s8[8388608]{0:T(1024)(128)(4,1)} %bitcast.81), calls=%async_computation | async-start | bytes 8388608
  352.1 8.3 %slice-start.1 = ((s8[8388608]{0:T(1024)(128)(4,1)}), s8[4194304]{0:T(1024)(128)(4,1)S(1)}, s32[]{:S(2)}) async-start(s8[8388608]{0:T(1024)(128)(4,1)} %bitcast.81), calls=%async_computation.1 | async-start | bytes 8388608
  352.2 15.0 %collective-permute-start.20 = (bf16[16,4,64,128]{3,2,1,0:T(8,128)(2,1)S(1)}, bf16[16,4,64,128]{3,2,1,0:T(8,128)(2,1)S(1)}, u32[]{:S(2)}, u32[]{:S(2)}) collective-permute-start(bf16[16,4,64,128]{3,2,1,0:T(8,128)(2,1)S(1)} %slice.130), channel_id=1, source_target_pairs={{0,2},{2,0},{4,6},{6,4},{1,3},{3,1},{5,7},{7,5},{8,10},{10,8},{12,... | collective-permute-start | bytes 3145736 | tf_op jit(solution)/shard_map/ppermute | solution.py:894
  359.7 65.4 %collective-permute-start.26 = (bf16[8,2,128,512]{3,2,1,0:T(8,128)(2,1)}, bf16[8,2,128,512]{3,2,1,0:T(8,128)(2,1)S(1)}, u32[]{:S(2)}, u32[]{:S(2)}) collective-permute-start(bf16[8,2,128,512]{3,2,1,0:T(8,128)(2,1)} %slice.182), channel_id=1, source_target_pairs={{0,1},{1,0},{2,3},{3,2},{4,5},{5,4},{6,7},{7,6},{8,9},{9,8},{10,11... | collective-permute-start | bytes 6291464 | tf_op jit(solution)/shard_map/ppermute | solution.py:894
  365.6 63.2 %collective-permute-start.31 = (bf16[8,2,128,512]{3,2,1,0:T(8,128)(2,1)}, bf16[8,2,128,512]{3,2,1,0:T(8,128)(2,1)}, u32[]{:S(2)}, u32[]{:S(2)}) collective-permute-start(bf16[8,2,128,512]{3,2,1,0:T(8,128)(2,1)} %slice.190), channel_id=1, source_target_pairs={{0,4},{2,6},{4,0},{6,2},{1,5},{3,7},{5,1},{7,3},{8,12},{10,14},{12... | collective-permute-start | bytes 6291464 | tf_op jit(solution)/shard_map/ppermute | solution.py:894
  368.5 54.4 %collective-permute-start.21 = (bf16[8,4,64,128]{3,2,1,0:T(8,128)(2,1)}, bf16[8,4,64,128]{3,2,1,0:T(8,128)(2,1)}, u32[]{:S(2)}, u32[]{:S(2)}) collective-permute-start(bf16[8,4,64,128]{3,2,1,0:T(8,128)(2,1)} %slice.171), channel_id=1, source_target_pairs={{0,1},{1,0},{2,3},{3,2},{4,5},{5,4},{6,7},{7,6},{8,9},{9,8},{10,11... | collective-permute-start | bytes 1572872 | tf_op jit(solution)/shard_map/ppermute | solution.py:894
  369.8 5.1 collective-permute-start.15
  375.0 5.2 collective-permute-start.16
  380.2 33.1 %collective-permute-start.17 = (f32[8,512]{1,0:T(8,128)S(1)}, f32[8,512]{1,0:T(8,128)S(1)}, u32[]{:S(2)}, u32[]{:S(2)}) collective-permute-start(f32[8,512]{1,0:T(8,128)S(1)} %add.227), channel_id=1, source_target_pairs={{0,4},{2,6},{4,0},{6,2},{1,5},{3,7},{5,1},{7,3},{8,12},{10,14},{12... | collective-permute-start | bytes 49160 | tf_op jit(solution)/shard_map/ppermute | solution.py:894
  413.3 5.5 %collective-permute-start.18 = (f32[8,512]{1,0:T(8,128)S(1)}, f32[8,512]{1,0:T(8,128)S(1)}, u32[]{:S(2)}, u32[]{:S(2)}) collective-permute-start(f32[8,512]{1,0:T(8,128)S(1)} %add.228), channel_id=1, source_target_pairs={{0,1},{1,0},{2,3},{3,2},{4,5},{5,4},{6,7},{7,6},{8,9},{9,8},{10,11... | collective-permute-start | bytes 49160 | tf_op jit(solution)/shard_map/ppermute | solution.py:894
  418.8 4.1 collective-permute-start.19
  424.2 9.2 %collective-permute-start.22 = (bf16[4,4,64,128]{3,2,1,0:T(8,128)(2,1)S(1)}, bf16[4,4,64,128]{3,2,1,0:T(8,128)(2,1)S(1)}, u32[]{:S(2)}, u32[]{:S(2)}) collective-permute-start(bf16[4,4,64,128]{3,2,1,0:T(8,128)(2,1)S(1)} %slice.173), channel_id=1, source_target_pairs={{0,4},{2,6},{4,0},{6,2},{1,5},{3,7},{5,1},{7,3},{8,12},{10,14},{12... | collective-permute-start | bytes 786440 | tf_op jit(solution)/shard_map/ppermute | solution.py:894
  427.9 27.6 %collective-permute-start.27 = (bf16[4,2,128,512]{3,2,1,0:T(8,128)(2,1)S(1)}, bf16[4,2,128,512]{3,2,1,0:T(8,128)(2,1)S(1)}, u32[]{:S(2)}, u32[]{:S(2)}) collective-permute-start(bf16[4,2,128,512]{3,2,1,0:T(8,128)(2,1)S(1)} %slice.184), channel_id=1, source_target_pairs={{0,4},{2,6},{4,0},{6,2},{1,5},{3,7},{5,1},{7,3},{8,12},{10,14},{12... | collective-permute-start | bytes 3145736 | tf_op jit(solution)/shard_map/ppermute | solution.py:894
  431.2 25.3 %collective-permute-start.32 = (bf16[4,2,128,512]{3,2,1,0:T(8,128)(2,1)S(1)}, bf16[4,2,128,512]{3,2,1,0:T(8,128)(2,1)S(1)}, u32[]{:S(2)}, u32[]{:S(2)}) collective-permute-start(bf16[4,2,128,512]{3,2,1,0:T(8,128)(2,1)S(1)} %slice.192), channel_id=1, source_target_pairs={{0,1},{1,0},{2,3},{3,2},{4,5},{5,4},{6,7},{7,6},{8,9},{9,8},{10,11... | collective-permute-start | bytes 3145736 | tf_op jit(solution)/shard_map/ppermute | solution.py:894
  433.5 5.9 %collective-permute-start.23 = (bf16[2,4,64,128]{3,2,1,0:T(8,128)(2,1)S(1)}, bf16[2,4,64,128]{3,2,1,0:T(8,128)(2,1)S(1)}, u32[]{:S(2)}, u32[]{:S(2)}) collective-permute-start(bf16[2,4,64,128]{3,2,1,0:T(8,128)(2,1)S(1)} %slice.175), channel_id=1, source_target_pairs={{0,16},{8,24},{16,0},{24,8},{1,17},{9,25},{17,1},{25,9},{2,18},{10... | collective-permute-start | bytes 393224 | tf_op jit(solution)/shard_map/ppermute | solution.py:894
  439.5 19.8 %copy-start.30 = (f32[64,3,128]{2,0,1:T(8,128)S(1)}, f32[64,3,128]{2,0,1:T(8,128)}, u32[]{:S(2)}) copy-start(f32[64,3,128]{2,0,1:T(8,128)} %param.29) | copy-start | bytes 294916
  439.5 19.8 %copy-start.33 = (f32[64,3,128]{2,0,1:T(8,128)S(1)}, f32[64,3,128]{2,0,1:T(8,128)}, u32[]{:S(2)}) copy-start(f32[64,3,128]{2,0,1:T(8,128)} %param.30) | copy-start | bytes 294916
  439.5 19.8 %copy-start.34 = (f32[64,3,128]{2,0,1:T(8,128)S(1)}, f32[64,3,128]{2,0,1:T(8,128)}, u32[]{:S(2)}) copy-start(f32[64,3,128]{2,0,1:T(8,128)} %param.31) | copy-start | bytes 294916
  439.5 19.8 %collective-permute-start.24 = (bf16[1,4,64,128]{3,2,1,0:T(8,128)(2,1)S(1)}, bf16[1,4,64,128]{3,2,1,0:T(8,128)(2,1)S(1)}, u32[]{:S(2)}, u32[]{:S(2)}) collective-permute-start(bf16[1,4,64,128]{3,2,1,0:T(8,128)(2,1)S(1)} %slice.177), channel_id=1, source_target_pairs={{0,8},{8,0},{16,24},{24,16},{1,9},{9,1},{17,25},{25,17},{2,10},{10... | collective-permute-start | bytes 196616 | tf_op jit(solution)/shard_map/ppermute | solution.py:894
  455.8 48.6 %copy-start.32 = (f32[128,64]{0,1:T(8,128)S(1)}, f32[128,64]{0,1:T(8,128)}, u32[]{:S(2)}) copy-start(f32[128,64]{0,1:T(8,128)} %param.32) | copy-start | bytes 98308
  455.8 48.6 %copy-start.35 = (f32[128,64]{0,1:T(8,128)S(1)}, f32[128,64]{0,1:T(8,128)}, u32[]{:S(2)}) copy-start(f32[128,64]{0,1:T(8,128)} %param.33) | copy-start | bytes 98308
  455.8 48.6 %copy-start.36 = (f32[128,64]{0,1:T(8,128)S(1)}, f32[128,64]{0,1:T(8,128)}, u32[]{:S(2)}) copy-start(f32[128,64]{0,1:T(8,128)} %param.34) | copy-start | bytes 98308
  455.8 38.3 %collective-permute-start.28 = (bf16[2,2,128,512]{3,2,1,0:T(8,128)(2,1)S(1)}, bf16[2,2,128,512]{3,2,1,0:T(8,128)(2,1)S(1)}, u32[]{:S(2)}, u32[]{:S(2)}) collective-permute-start(bf16[2,2,128,512]{3,2,1,0:T(8,128)(2,1)S(1)} %slice.186), channel_id=1, source_target_pairs={{0,16},{8,24},{16,0},{24,8},{1,17},{9,25},{17,1},{25,9},{2,18},{10... | collective-permute-start | bytes 1572872 | tf_op jit(solution)/shard_map/ppermute | solution.py:894
  456.9 58.6 %copy-start.17 = (f32[1,1024,128]{1,2,0:T(8,128)S(1)}, f32[1,1024,128]{1,2,0:T(8,128)}, u32[]{:S(2)}) copy-start(f32[1,1024,128]{1,2,0:T(8,128)} %copy-done.16) | copy-start | bytes 1572868
  456.9 58.6 %copy-start.25 = (f32[1,1024,128]{1,2,0:T(8,128)S(1)}, f32[1,1024,128]{1,2,0:T(8,128)}, u32[]{:S(2)}) copy-start(f32[1,1024,128]{1,2,0:T(8,128)} %copy.82) | copy-start | bytes 1572868
  456.9 58.6 %copy-start.26 = (f32[1,1024,128]{1,2,0:T(8,128)S(1)}, f32[1,1024,128]{1,2,0:T(8,128)}, u32[]{:S(2)}) copy-start(f32[1,1024,128]{1,2,0:T(8,128)} %copy.83) | copy-start | bytes 1572868
  456.9 47.2 %collective-permute-start.33 = (bf16[2,2,128,512]{3,2,1,0:T(8,128)(2,1)S(1)}, bf16[2,2,128,512]{3,2,1,0:T(8,128)(2,1)S(1)}, u32[]{:S(2)}, u32[]{:S(2)}) collective-permute-start(bf16[2,2,128,512]{3,2,1,0:T(8,128)(2,1)S(1)} %slice.194), channel_id=1, source_target_pairs={{0,16},{8,24},{16,0},{24,8},{1,17},{9,25},{17,1},{25,9},{2,18},{10... | collective-permute-start | bytes 1572872 | tf_op jit(solution)/shard_map/ppermute | solution.py:894
  494.3 15.5 %collective-permute-start.29 = (bf16[1,2,128,512]{3,2,1,0:T(8,128)(2,1)S(1)}, bf16[1,2,128,512]{3,2,1,0:T(8,128)(2,1)S(1)}, u32[]{:S(2)}, u32[]{:S(2)}) collective-permute-start(bf16[1,2,128,512]{3,2,1,0:T(8,128)(2,1)S(1)} %slice.188), channel_id=1, source_target_pairs={{0,8},{8,0},{16,24},{24,16},{1,9},{9,1},{17,25},{25,17},{2,10},{10... | collective-permute-start | bytes 786440 | tf_op jit(solution)/shard_map/ppermute | solution.py:894
  504.3 11.0 %collective-permute-start.34 = (bf16[1,2,128,512]{3,2,1,0:T(8,128)(2,1)S(1)}, bf16[1,2,128,512]{3,2,1,0:T(8,128)(2,1)S(1)}, u32[]{:S(2)}, u32[]{:S(2)}) collective-permute-start(bf16[1,2,128,512]{3,2,1,0:T(8,128)(2,1)S(1)} %slice.196), channel_id=1, source_target_pairs={{0,8},{8,0},{16,24},{24,16},{1,9},{9,1},{17,25},{25,17},{2,10},{10... | collective-permute-start | bytes 786440 | tf_op jit(solution)/shard_map/ppermute | solution.py:894
  (25 other events, 94.3 us)
